TPU v7x, 512 devices: a whole 4x8x8 slice. The times are simulated.
512 devices in a mesh: orient: 8 (over z_lo, x), tile: 64 (over y, z_hi, core).
Axes of the slice: x: 4, y: 8, z: 8 (z_hi: 4, z_lo: 2; z = z_hi * 2 + z_lo), core: 2. Of those that a mesh axis runs over, the one named last changes fastest.
Arguments:
- image_tiles: bfloat16 [64, 512, 512], P('tile'), may hold values from -6 to 6
- templates: bfloat16 [8, 64, 384, 384], P('orient', 'tile'), may hold values from -0.015625 to 0.015625
- owners: int32 [8, 2], P('orient'), may hold values from 0 to 63, as said below
Outputs:
- corr_sum: float32 [64, 512, 512], P('tile', 'orient')
- corr_sumsq: float32 [64, 512, 512], P('tile', 'orient')
- corr_max: float32 [64, 512, 512], P('tile', 'orient')
Inputs may be any that keep to these rules, and one draw needn't show every extreme that they name: Within a group the 2 owners are distinct.
All inputs are finite; a program needn't handle non-finite values.
Results may differ from a plain program's by a relative error of at most 0.02.
Values may be sent and summed in bfloat16 or wider, within the bound.
No kernel may reach another device: no remote copies, remote signals or barrier semaphores. Data moves between devices by JAX's collectives and lax.ppermute only.
A program may use at most 64 MiB of HBM per device.

v0:
```python
import jax
import jax.numpy as jnp
from jax import lax
from jax.sharding import PartitionSpec as P

STEPS = 2


def broadcast(block, axis, source):
    block = jnp.where(lax.axis_index(axis) == source, block, jnp.zeros_like(block))
    return lax.psum(block, axis)


def make_tables(size):
    index_line = jnp.arange(size, dtype=jnp.int32)
    phases = index_line[:, None] * index_line[None, :] % size
    angles = phases.astype(jnp.float32) * (2.0 * 3.141592653589793 / size)
    return (jnp.cos(angles).astype(jnp.bfloat16), jnp.sin(angles).astype(jnp.bfloat16))


def matmul(left, right):
    return jnp.dot(left, right, preferred_element_type=jnp.float32)


def forward_image(field, cos_table, sin_table):
    first_a = matmul(cos_table, field).astype(jnp.bfloat16)
    first_b = matmul(sin_table, field).astype(jnp.bfloat16)
    spec_re = (matmul(first_a, cos_table) - matmul(first_b, sin_table)).astype(jnp.bfloat16)
    spec_im = (-(matmul(first_a, sin_table) + matmul(first_b, cos_table))).astype(jnp.bfloat16)
    return (spec_re, spec_im)


def forward_template(template, cos_table, sin_table):
    width = template.shape[0]
    cos_left = cos_table[:, :width]
    sin_left = sin_table[:, :width]
    first_a = matmul(cos_left, template).astype(jnp.bfloat16)
    first_b = matmul(sin_left, template).astype(jnp.bfloat16)
    cos_top = cos_table[:width, :]
    sin_top = sin_table[:width, :]
    spec_re = (matmul(first_a, cos_top) - matmul(first_b, sin_top)).astype(jnp.bfloat16)
    spec_im = (-(matmul(first_a, sin_top) + matmul(first_b, cos_top))).astype(jnp.bfloat16)
    return (spec_re, spec_im)


def correlate(image_re, image_im, tmpl_re, tmpl_im, cos_table, sin_table):
    size = image_re.shape[0]
    ire = image_re.astype(jnp.float32)
    iim = image_im.astype(jnp.float32)
    tre = tmpl_re.astype(jnp.float32)
    tim = tmpl_im.astype(jnp.float32)
    prod_re = (ire * tre + iim * tim).astype(jnp.bfloat16)
    prod_im = (iim * tre - ire * tim).astype(jnp.bfloat16)
    back_re = (matmul(cos_table, prod_re) - matmul(sin_table, prod_im)).astype(jnp.bfloat16)
    back_im = (matmul(cos_table, prod_im) + matmul(sin_table, prod_re)).astype(jnp.bfloat16)
    scale = jnp.float32(1.0 / (size * size))
    return (matmul(back_re, cos_table) - matmul(back_im, sin_table)) * scale


def per_device(image_tiles, templates, owners):
    field = image_tiles[0]
    own_template = templates[0, 0]
    size = field.shape[0]
    cos_table, sin_table = make_tables(size)
    image_re, image_im = forward_image(field, cos_table, sin_table)
    groups_here = lax.axis_size("orient")
    rows_out = size // groups_here
    total = jnp.zeros((size, size), jnp.float32)
    squares = jnp.zeros((size, size), jnp.float32)
    largest = jnp.full((size, size), -jnp.inf, jnp.float32)
    for step_index in range(STEPS):
        root_index = owners[0, step_index]
        received = broadcast(own_template, "tile", root_index)
        tmpl_re, tmpl_im = forward_template(received, cos_table, sin_table)
        values = correlate(image_re, image_im, tmpl_re, tmpl_im, cos_table, sin_table)
        largest = jnp.maximum(largest, values)
        total = total + values
        squares = squares + values * values
    shared_total, shared_squares = (
        lax.psum_scatter(
            total.astype(jnp.bfloat16), "orient", scatter_dimension=0, tiled=True
        ).astype(jnp.float32),
        lax.psum_scatter(
            squares.astype(jnp.bfloat16), "orient", scatter_dimension=0, tiled=True
        ).astype(jnp.float32),
    )
    everywhere = lax.pmax(largest.astype(jnp.bfloat16), "orient").astype(largest.dtype)
    start_row = lax.axis_index("orient") * rows_out
    shared_max = lax.dynamic_slice_in_dim(everywhere, start_row, rows_out, 0)
    return (shared_total[None], shared_squares[None], shared_max[None])


def solution(mesh):
    placed = (P("tile", None, None), P("orient", "tile", None, None), P("orient", None))
    return jax.shard_map(
        per_device,
        mesh=mesh,
        in_specs=placed,
        out_specs=(P("tile", "orient", None), P("tile", "orient", None), P("tile", "orient", None)),
        check_vma=False,
    )
```

profile of v0, /device:TPU:1, one launch (start us, length us, event | category | flops | bytes accessed | tf_op | source)
XLA Modules:
  0.0 766.6 jit_solution(874491180624757986)
XLA Ops:
  7.2 0.0 all-reduce.6.cloned.1.call-start
  7.2 0.7 copy-done.6
  7.9 0.6 fusion.127
  9.8 1.8 select_bitcast_fusion
  11.6 0.0 all-reduce.6.cloned.1.call-update
  11.7 0.0 all-reduce.4.cloned.1.call-start
  11.7 4.4 convolution_convert_fusion.1
  16.2 4.5 convolution_convert_fusion
  20.6 3.9 cosine_convert_fusion
  24.6 4.0 sine_convert_fusion
  28.5 4.8 fusion.37
  33.4 4.9 fusion.38
  38.2 5.0 fusion.5
  43.2 5.4 fusion.7
  48.7 489.0 %all-reduce.6.cloned.1.call-done = (bf16[384,384]{1,0:T(8,128)(2,1)}, bf16[384,384]{1,0:T(8,128)(2,1)}) async-done(((bf16[384,384]{1,0:T(8,128)(2,1)}, bf16[384,384]{1,0:T(8,128)(2,1)}), (bf16[384,384]{1,0:T(8,128)(2,1)}, bf16[384,384]{1,0:T(8,128)(2,1)})) %all-reduce.6.cloned.1.call-update) | async-done | bytes 589840 | tf_op jit(solution)/shard_map/psum | solution.py:11
  537.7 1.4 convolution_convert_fusion.3
  539.1 0.4 convolution_convert_fusion.2
  539.5 0.5 copy-done.1
  540.1 0.4 convolution_convert_fusion.5
  540.5 0.4 convolution_convert_fusion.4
  540.9 0.4 fusion.46
  541.3 0.4 fusion.53
  541.7 0.4 fusion.50
  542.2 0.4 fusion.43
  542.6 0.4 fusion.8
  543.0 0.4 fusion.6
  543.5 0.4 fusion.11
  543.9 1.8 fusion.27
  545.7 3.9 fusion.36
  549.6 5.3 fusion.35
  554.9 5.6 fusion.16
  560.5 3.9 fusion.34
  564.4 5.3 fusion.33
  569.8 5.6 fusion.15
  575.4 5.9 fusion.2
  581.3 7.0 add_convert_fusion
  588.2 1.0 max.7
  589.2 0.0 all-reduce.4.cloned.1.call-update
  589.2 0.0 reduce-scatter.3.cloned.1.call-start
  589.3 0.7 reduce-scatter.3.cloned.1.call-update
  589.9 0.0 reduce-scatter.5.cloned.1.call-start
  590.0 0.5 reduce-scatter.5.cloned.1.call-update
  590.5 77.2 %all-reduce.4.cloned.1.call-done = bf16[512,512]{1,0:T(8,128)(2,1)} async-done(((bf16[512,512]{1,0:T(8,128)(2,1)}), bf16[512,512]{1,0:T(8,128)(2,1)}) %all-reduce.4.cloned.1.call-update) | async-done | bytes 524304 | tf_op jit(solution)/shard_map/pmax | solution.py:87
  667.7 1.5 convert_bitcast_fusion
  669.2 44.6 %reduce-scatter.3.cloned.1.call-done = bf16[64,512]{1,0:T(8,128)(2,1)} async-done(((bf16[512,512]{1,0:T(8,128)(2,1)}), bf16[64,512]{1,0:T(8,128)(2,1)}) %reduce-scatter.3.cloned.1.call-update) | async-done | bytes 65552 | tf_op jit(solution)/shard_map/reduce_scatter | solution.py:80
  713.8 1.5 bitcast_convert_fusion.1
  715.3 43.0 %reduce-scatter.5.cloned.1.call-done = bf16[64,512]{1,0:T(8,128)(2,1)} async-done(((bf16[512,512]{1,0:T(8,128)(2,1)}), bf16[64,512]{1,0:T(8,128)(2,1)}) %reduce-scatter.5.cloned.1.call-update) | async-done | bytes 65552 | tf_op jit(solution)/shard_map/reduce_scatter | solution.py:83
  758.3 1.5 bitcast_convert_fusion
  (12 shorter events, 0.0 us)
Async XLA Ops:
  7.2 4.6 copy-start
  7.2 530.5 %all-reduce.6.cloned.1.call-start = ((), (), s32[]{:S(2)}) async-start(), calls=%async_computation.5 | async-start | bytes 1179648 | tf_op jit(solution)/shard_map/psum | solution.py:11
  7.2 0.7 copy-start.6
  11.7 656.0 %all-reduce.4.cloned.1.call-start = ((), (), s32[]{:S(2)}) async-start(), calls=%async_computation.4 | async-start | bytes 1048576 | tf_op jit(solution)/shard_map/pmax | solution.py:87
  537.7 1.4 copy-start.2
  539.1 1.0 copy-start.1
  545.7 3.9 copy-start.3
  560.5 3.9 copy-start.5
  569.8 5.6 copy-start.4
  589.2 124.6 %reduce-scatter.3.cloned.1.call-start = ((), (), s32[]{:S(2)}) async-start(), calls=%async_computation.2 | async-start | bytes 589824 | tf_op jit(solution)/shard_map/reduce_scatter | solution.py:80
  589.9 168.4 %reduce-scatter.5.cloned.1.call-start = ((), (), s32[]{:S(2)}) async-start(), calls=%async_computation.3 | async-start | bytes 589824 | tf_op jit(solution)/shard_map/reduce_scatter | solution.py:83
Sparse Core Ops, SparseCore 0:
  11.8 525.8 all-reduce.5
  589.3 78.3 all-reduce.3
  670.7 42.9 reduce-scatter.2
  716.4 41.8 reduce-scatter.4
where the time goes:
time: 779 us; the launch traced here: 767 us
  waiting for transfers between devices  655 us (84%)
  matrix products  78.9 us (10%)
  between operations  15.5 us (2%)
  other arithmetic  15.2 us (2%)
    psum x1, waiting for transfers between devices, broadcast(): return lax.psum(block, axis)  489 us
    dot_general x26, matrix products, matmul(): return jnp.dot(left, right, preferred_element_type=jnp.float32)  78.9 us
    pmax x1, waiting for transfers between devices, per_device(): lax.pmax(largest.astype(jnp.bfloat16), 'orient').astype(largest.dtype)  77.2 us
    reduce_scatter x1, waiting for transfers between devices, per_device(): lax.psum_scatter(total.astype(jnp.bfloat16), 'orient', scatter_dimension=...  44.6 us
    reduce_scatter x1, waiting for transfers between devices, per_device(): lax.psum_scatter(squares.astype(jnp.bfloat16), 'orient', scatter_dimensio...  43 us
  transfers between devices with their start and end apart: 4, of which 4 were waited for; matrix products, arithmetic and copies ran while one was open for 5% of the time, Pallas kernels for 0%

commit v1 on v0

v1 whole, which is shorter than its diff:
```python
import numpy as np
import jax
import jax.numpy as jnp
from jax import lax
from jax.experimental import pallas as pl
from jax.experimental.pallas import tpu as pltpu
from jax.sharding import PartitionSpec as P

STEPS = 2
NP = 512
HALF = NP // 2
M = 384
REST = M - HALF
Y, Z, CORES = 8, 4, 2
PLANE = Y * CORES
CHUNK = M // PLANE


def make_tables():
    line = np.arange(NP)
    phases = (line[:, None] * line[None, :]) % NP
    angles = phases.astype(np.float32) * np.float32(2.0 * 3.141592653589793 / NP)
    cos_table, sin_table = np.cos(angles), np.sin(angles)
    tables = []
    for parity in (0, 1):
        cos_part = cos_table[parity::2, :HALF]
        sin_part = sin_table[parity::2, :HALF]
        tables.append(np.block([[cos_part, sin_part], [-sin_part, cos_part]]))
    tables = np.stack(tables).astype(jnp.bfloat16)
    return tables, np.ascontiguousarray(tables.transpose(0, 2, 1))


def matmul(left, right):
    return jnp.dot(left, right, preferred_element_type=jnp.float32)


def right_transform(stacked, table):
    return matmul(stacked[:HALF], table[:HALF]) + matmul(stacked[HALF:], table[HALF:])


def wide(values):
    return values.astype(jnp.float32)


def narrow(values):
    return values.astype(jnp.bfloat16)


def combine(left, right, parity):
    return left + right if parity == 0 else left - right


def image_kernel(field_ref, fwd_ref, inv_ref, spec_ref):
    top_left, top_right = wide(field_ref[:HALF, :HALF]), wide(field_ref[:HALF, HALF:])
    low_left, low_right = wide(field_ref[HALF:, :HALF]), wide(field_ref[HALF:, HALF:])
    for row_parity in (0, 1):
        left = combine(top_left, low_left, row_parity)
        right = combine(top_right, low_right, row_parity)
        for col_parity in (0, 1):
            folded = narrow(combine(left, right, col_parity))
            first = narrow(matmul(fwd_ref[row_parity, :, :HALF], folded))
            spec_ref[row_parity, col_parity] = narrow(right_transform(first, inv_ref[col_parity]))


def correlate_kernel(parts_ref, spec_ref, fwd_ref, inv_ref, out_ref, field_ref, back_ref):
    for step in range(STEPS):
        for part in range(PLANE):
            rows = slice(part * CHUNK, (part + 1) * CHUNK)
            values = wide(parts_ref[part, step])
            field_ref[step, rows, :] = values if step == 0 else -values
    for row_parity in (0, 1):
        rows_folded = []
        for step in range(STEPS):
            top = combine(field_ref[step, :REST], field_ref[step, HALF:], row_parity)
            rows_folded.append((top, field_ref[step, REST:HALF]))
        for col_parity in (0, 1):
            pieces = []
            for step in range(STEPS):
                for block in rows_folded[step]:
                    left = combine(block[:, :REST], block[:, HALF:], col_parity)
                    pieces.append(narrow(jnp.concatenate([left, block[:, REST:HALF]], axis=1)))
            first = narrow(matmul(fwd_ref[row_parity], jnp.concatenate(pieces, axis=0)))
            tmpl = right_transform(first, inv_ref[col_parity])
            tmpl_re, tmpl_im = tmpl[:, :HALF], tmpl[:, HALF:]
            image_re = wide(spec_ref[row_parity, col_parity, :, :HALF])
            image_im = wide(spec_ref[row_parity, col_parity, :, HALF:])
            prod_re = narrow(image_re * tmpl_re + image_im * tmpl_im)
            prod_im = narrow(image_im * tmpl_re - image_re * tmpl_im)
            back = narrow(matmul(inv_ref[row_parity], jnp.concatenate([prod_re, prod_im], axis=0)))
            back_ref[row_parity, col_parity] = right_transform(back, fwd_ref[col_parity])
    blocks, _, rows_out, _ = out_ref.shape
    for step in range(STEPS):
        cols = slice(step * HALF, (step + 1) * HALF)
        for block in range(blocks // 2):
            rows = slice(block * rows_out, (block + 1) * rows_out)
            even_even, even_odd = back_ref[0, 0, rows, cols], back_ref[0, 1, rows, cols]
            odd_even, odd_odd = back_ref[1, 0, rows, cols], back_ref[1, 1, rows, cols]
            even_left, odd_left = even_even + even_odd, odd_even + odd_odd
            even_right, odd_right = even_even - even_odd, odd_even - odd_odd
            out_ref[block, step, :, :HALF] = narrow(even_left + odd_left)
            out_ref[block, step, :, HALF:] = narrow(even_right + odd_right)
            out_ref[block + blocks // 2, step, :, :HALF] = narrow(even_left - odd_left)
            out_ref[block + blocks // 2, step, :, HALF:] = narrow(even_right - odd_right)


def statistics_kernel(values_ref, total_ref, squares_ref, largest_ref):
    scale = jnp.float32(1.0 / (NP * NP))
    total = squares = largest = None
    for group in range(values_ref.shape[0]):
        for step in range(STEPS):
            values = wide(values_ref[group, step]) * scale
            if total is None:
                total, squares, largest = values, values * values, values
            else:
                total = total + values
                squares = squares + values * values
                largest = jnp.maximum(largest, values)
    total_ref[0] = total
    squares_ref[0] = squares
    largest_ref[0] = largest


def call(kernel, name, outs, scratch, *operands):
    whole = pl.BlockSpec(memory_space=pltpu.VMEM)
    return pl.pallas_call(
        kernel,
        name=name,
        out_shape=outs,
        in_specs=[whole] * len(operands),
        out_specs=jax.tree.map(lambda _: whole, outs),
        scratch_shapes=scratch,
        compiler_params=pltpu.CompilerParams(vmem_limit_bytes=32 * 1024 * 1024),
    )(*operands)


def share_templates(own_template, owners):
    tile_index = lax.axis_index("tile")
    planes = [[(y * Z + z) * CORES + c for y in range(Y) for c in range(CORES)] for z in range(Z)]
    columns = [[(y * Z + z) * CORES + c for z in range(Z)] for y in range(Y) for c in range(CORES)]
    owner_z = owners // CORES % Z
    owner_place = owners // (Z * CORES) * CORES + owners % CORES
    shares = lax.all_to_all(
        own_template.reshape(PLANE, CHUNK, M), "tile", 0, 0, axis_index_groups=planes
    )
    kept = jnp.stack([shares[owner_place[step]] for step in range(STEPS)])
    spread = jnp.broadcast_to(kept[None], (Z, *kept.shape))
    spread = lax.all_to_all(spread, "tile", 0, 0, axis_index_groups=columns)
    kept = jnp.stack([spread[owner_z[step], step] for step in range(STEPS)])
    spread = jnp.broadcast_to(kept[None], (PLANE, *kept.shape))
    return lax.all_to_all(spread, "tile", 0, 0, axis_index_groups=planes)


def per_device(image_tiles, templates, owners):
    fwd, inv = (jnp.asarray(table) for table in make_tables())
    groups_here = lax.axis_size("orient")
    rows_out = NP // groups_here
    quarter = (2, 2, HALF, NP)
    spec = call(
        image_kernel, "image_spectrum", jax.ShapeDtypeStruct(quarter, jnp.bfloat16), [], image_tiles[0], fwd, inv
    )
    parts = share_templates(templates[0, 0], owners[0])
    values = call(
        correlate_kernel,
        "correlate",
        jax.ShapeDtypeStruct((groups_here, STEPS, rows_out, NP), jnp.bfloat16),
        [pltpu.VMEM((STEPS, M, M), jnp.float32), pltpu.VMEM(quarter, jnp.float32)],
        parts,
        spec,
        fwd,
        inv,
    )
    values = lax.all_to_all(values, "orient", 0, 0)
    out = jax.ShapeDtypeStruct((1, rows_out, NP), jnp.float32)
    return call(statistics_kernel, "statistics", (out, out, out), [], values)


def solution(mesh):
    placed = (P("tile", None, None), P("orient", "tile", None, None), P("orient", None))
    return jax.shard_map(
        per_device,
        mesh=mesh,
        in_specs=placed,
        out_specs=(P("tile", "orient", None), P("tile", "orient", None), P("tile", "orient", None)),
        check_vma=False,
    )
```

time: 779 us -> 92.6 us (0.12); the launches traced: 767 us -> 92 us
  waiting for transfers between devices: 655 us -> 28.9 us
  matrix products: 78.9 us -> 0 us
  starting transfers between devices: 0.16 us -> 24.2 us
  blocking collectives: 0 us -> 19.4 us
  other arithmetic: 15.2 us -> 0.04 us
  Pallas kernels: 0 us -> 7.99 us
    psum x1 -> x0, waiting for transfers between devices: 489 us -> none  [broadcast(): return lax.psum(block, axis)]
    reduce_scatter x2 -> x0, waiting for transfers between devices: 87.6 us -> none  [the longest x1 44.6 us: per_device(): lax.psum_scatter(total.astype(jnp.bfloat16), 'orient', scatter_dimension=...]
    dot_general x26 -> x0, matrix products: 78.9 us -> none  [matmul(): return jnp.dot(left, right, preferred_element_type=jnp.float32)]
    pmax x1 -> x0, waiting for transfers between devices: 77.2 us -> none  [per_device(): lax.pmax(largest.astype(jnp.bfloat16), 'orient').astype(largest.dtype)]
    all_to_all x0 -> x3, waiting for transfers between devices: none -> 28.9 us  [the longest x1 16.4 us: share_templates(): return lax.all_to_all(spread, 'tile', 0, 0, axis_index_groups=planes)]
    all_to_all x0 -> x3, starting transfers between devices: none -> 24.2 us  [the longest x1 10.2 us: share_templates(): lax.all_to_all(own_template.reshape(PLANE, CHUNK, M), 'tile', 0, 0, axis_...]
    all_to_all x0 -> x1, blocking collectives: none -> 19.4 us  [per_device(): values = lax.all_to_all(values, 'orient', 0, 0)]
    pallas_call x0 -> x3, Pallas kernels: none -> 7.99 us  [call(): pl.pallas_call(kernel, name=name, out_shape=outs, in_specs=[whole] * len(...]
  transfers between devices with their start and end apart: 4 -> 3, of which waited for: 4 -> 3; matrix products, arithmetic and copies ran while one was open for 5% -> 1% of each run, Pallas kernels for 0% -> 1%
where the time goes in v1:
time: 92.6 us; the launch traced here: 92 us
  waiting for transfers between devices  28.9 us (31%)
  starting transfers between devices  24.2 us (26%)
  blocking collectives  19.4 us (21%)
  between operations  8.29 us (9%)
  Pallas kernels  7.99 us (9%)
  local copies, waits for them, and re-layouts  3.19 us (3%)
    all_to_all x1, blocking collectives, per_device(): values = lax.all_to_all(values, 'orient', 0, 0)  19.4 us
    all_to_all x1, waiting for transfers between devices, share_templates(): return lax.all_to_all(spread, 'tile', 0, 0, axis_index_groups=planes)  16.4 us
    all_to_all x1, starting transfers between devices, share_templates(): lax.all_to_all(own_template.reshape(PLANE, CHUNK, M), 'tile', 0, 0, axis_...  10.2 us
    all_to_all x1, starting transfers between devices, share_templates(): spread = lax.all_to_all(spread, 'tile', 0, 0, axis_index_groups=columns)  8.47 us
    all_to_all x1, waiting for transfers between devices, share_templates(): lax.all_to_all(own_template.reshape(PLANE, CHUNK, M), 'tile', 0, 0, axis_...  8.22 us
    pallas_call x3, Pallas kernels, call(): pl.pallas_call(kernel, name=name, out_shape=outs, in_specs=[whole] * len(...  7.99 us
    all_to_all x1, starting transfers between devices, share_templates(): return lax.all_to_all(spread, 'tile', 0, 0, axis_index_groups=planes)  5.51 us
    all_to_all x1, waiting for transfers between devices, share_templates(): spread = lax.all_to_all(spread, 'tile', 0, 0, axis_index_groups=columns)  4.32 us
  transfers between devices with their start and end apart: 3, of which 3 were waited for; matrix products, arithmetic and copies ran while one was open for 1% of the time, Pallas kernels for 1%

profile of v1, /device:TPU:1, one launch (start us, length us, event | category | flops | bytes accessed | tf_op | source)
XLA Modules:
  0.0 92.0 jit_solution(6612298451007727914)
XLA Ops:
  0.6 0.0 copy-start.3
  0.6 10.2 %all-to-all-start = ((bf16[16,24,384]{2,1,0:T(8,128)(2,1)}), bf16[16,24,384]{2,1,0:T(8,128)(2,1)S(1)}, u32[]{:S(2)}, u32[]{:S(2)}) async-start(bf16[16,24,384]{2,1,0:T(8,128)(2,1)} %bitcast.35), calls=%async_computation | async-start | bytes 589824 | tf_op jit(solution)/shard_map/all_to_all | solution.py:142
  10.9 0.0 copy-done.3
  10.9 0.6 fusion.2
  15.1 8.2 %all-to-all-done = bf16[16,24,384]{2,1,0:T(8,128)(2,1)S(1)} async-done(((bf16[16,24,384]{2,1,0:T(8,128)(2,1)}), bf16[16,24,384]{2,1,0:T(8,128)(2,1)S(1)}, u32[]{:S(2)}, u32[]{:S(2)}) %all-to-all-start) | async-done | bytes 294944 | tf_op jit(solution)/shard_map/all_to_all | solution.py:142
  23.3 0.7 broadcast_in_dim.4
  24.0 0.0 copy-start.1
  24.0 8.5 %all-to-all-start.1 = ((bf16[4,2,24,384]{3,2,1,0:T(8,128)(2,1)}), bf16[4,2,24,384]{3,2,1,0:T(8,128)(2,1)S(1)}, u32[]{:S(2)}, u32[]{:S(2)}) async-start(bf16[4,2,24,384]{3,2,1,0:T(8,128)(2,1)} %broadcast_in_dim.4), calls=%async_computation.1 | async-start | bytes 294912 | tf_op jit(solution)/shard_map/all_to_all | solution.py:147
  32.5 0.0 copy-start
  36.5 4.3 %all-to-all-done.1 = bf16[4,2,24,384]{3,2,1,0:T(8,128)(2,1)S(1)} async-done(((bf16[4,2,24,384]{3,2,1,0:T(8,128)(2,1)}), bf16[4,2,24,384]{3,2,1,0:T(8,128)(2,1)S(1)}, u32[]{:S(2)}, u32[]{:S(2)}) %all-to-all-start.1) | async-done | bytes 147488 | tf_op jit(solution)/shard_map/all_to_all | solution.py:147
  40.8 0.9 broadcast_in_dim.5
  41.7 5.5 %all-to-all-start.2 = ((bf16[16,2,24,384]{3,2,1,0:T(8,128)(2,1)}), bf16[16,2,24,384]{3,2,1,0:T(8,128)(2,1)}, u32[]{:S(2)}, u32[]{:S(2)}) async-start(bf16[16,2,24,384]{3,2,1,0:T(8,128)(2,1)} %broadcast_in_dim.5), calls=%async_computation.2 | async-start | bytes 1179648 | tf_op jit(solution)/shard_map/all_to_all | solution.py:150
  47.2 0.0 copy-done.1
  47.2 0.0 copy-done
  47.2 0.0 copy-start.2
  47.2 1.0 %copy-done.2 = bf16[1,512,512]{2,1,0:T(8,128)(2,1)S(1)} copy-done((bf16[1,512,512]{2,1,0:T(8,128)(2,1)S(1)}, bf16[1,512,512]{2,1,0:T(8,128)(2,1)}, u32[]{:S(2)}) %copy-start.2) | copy-done | bytes 524312
  48.2 1.3 %image_spectrum.1.spec_ref = bf16[2,2,256,512]{3,2,1,0:T(8,128)(2,1)S(1)} custom-call(bf16[512,512]{1,0:T(8,128)(2,1)S(1)} %bitcast.34, bf16[2,512,512]{2,1,0:T(8,128)(2,1)S(1)} %copy-done.1, bf16[2,512,512]{2,1,0:T(8,128)(2,1)S(1)} %copy-done), custom_call_target="tpu_custom_call" | custom-call | tf_op jit(solution)/shard_map/image_spectrum/pallas_call | solution.py:125
  49.5 16.4 %all-to-all-done.2.parts_ref = bf16[16,2,24,384]{3,2,1,0:T(8,128)(2,1)} async-done(((bf16[16,2,24,384]{3,2,1,0:T(8,128)(2,1)}), bf16[16,2,24,384]{3,2,1,0:T(8,128)(2,1)}, u32[]{:S(2)}, u32[]{:S(2)}) %all-to-all-start.2) | async-done | bytes 589856 | tf_op jit(solution)/shard_map/all_to_all | solution.py:150
  65.9 5.6 %correlate.1 = bf16[8,2,64,512]{3,2,1,0:T(8,128)(2,1)S(1)} custom-call(bf16[16,2,24,384]{3,2,1,0:T(8,128)(2,1)} %all-to-all-done.2.parts_ref, bf16[2,2,256,512]{3,2,1,0:T(8,128)(2,1)S(1)} %image_spectrum.1.spec_ref, bf16[2,512,512]{2,1,0:T(8,128)(2,1)S(1)} %copy-done.1, bf16[2,512,512]{2,1,0:T(8,128)(2,1)S(1)} %copy-done), custom_call_target="tpu_custom_call" | custom-call | tf_op jit(solution)/shard_map/correlate/pallas_call | solution.py:125
  71.5 19.4 %all_to_all.20.values_ref = bf16[8,2,64,512]{3,2,1,0:T(8,128)(2,1)S(1)} all-to-all(bf16[8,2,64,512]{3,2,1,0:T(8,128)(2,1)S(1)} %correlate.1), channel_id=1, replica_groups=mesh['orient'=8,'tile'=64] {'orient'}, dimensions={0} | all-to-all | bytes 2097152 | tf_op jit(solution)/shard_map/all_to_all | solution.py:172
  90.9 1.1 %statistics.1 = (f32[1,64,512]{2,1,0:T(8,128)}, f32[1,64,512]{2,1,0:T(8,128)}, f32[1,64,512]{2,1,0:T(8,128)}) custom-call(bf16[8,2,64,512]{3,2,1,0:T(8,128)(2,1)S(1)} %all_to_all.20.values_ref), custom_call_target="tpu_custom_call" | custom-call | tf_op jit(solution)/shard_map/statistics/pallas_call | solution.py:125
  (5 shorter events, 0.1 us)
Async XLA Ops:
  0.6 10.2 %copy-start.3 = (s32[1,2]{1,0:T(1,128)S(1)}, s32[1,2]{1,0:T(1,128)}, u32[]{:S(2)}) copy-start(s32[1,2]{1,0:T(1,128)} %param.7) | copy-start | bytes 28
  0.6 22.7 %all-to-all-start = ((bf16[16,24,384]{2,1,0:T(8,128)(2,1)}), bf16[16,24,384]{2,1,0:T(8,128)(2,1)S(1)}, u32[]{:S(2)}, u32[]{:S(2)}) async-start(bf16[16,24,384]{2,1,0:T(8,128)(2,1)} %bitcast.35), calls=%async_computation | async-start | bytes 589824 | tf_op jit(solution)/shard_map/all_to_all | solution.py:142
  24.0 23.2 %copy-start.1 = (bf16[2,512,512]{2,1,0:T(8,128)(2,1)S(1)}, bf16[2,512,512]{2,1,0:T(8,128)(2,1)}, u32[]{:S(2)}) copy-start(bf16[2,512,512]{2,1,0:T(8,128)(2,1)} %constant.56.clone.fwd_ref) | copy-start | bytes 3145732
  24.0 16.8 %all-to-all-start.1 = ((bf16[4,2,24,384]{3,2,1,0:T(8,128)(2,1)}), bf16[4,2,24,384]{3,2,1,0:T(8,128)(2,1)S(1)}, u32[]{:S(2)}, u32[]{:S(2)}) async-start(bf16[4,2,24,384]{3,2,1,0:T(8,128)(2,1)} %broadcast_in_dim.4), calls=%async_computation.1 | async-start | bytes 294912 | tf_op jit(solution)/shard_map/all_to_all | solution.py:147
  32.5 14.7 %copy-start = (bf16[2,512,512]{2,1,0:T(8,128)(2,1)S(1)}, bf16[2,512,512]{2,1,0:T(8,128)(2,1)}, u32[]{:S(2)}) copy-start(bf16[2,512,512]{2,1,0:T(8,128)(2,1)} %constant.57.clone.inv_ref) | copy-start | bytes 3145732
  41.7 24.3 %all-to-all-start.2 = ((bf16[16,2,24,384]{3,2,1,0:T(8,128)(2,1)}), bf16[16,2,24,384]{3,2,1,0:T(8,128)(2,1)}, u32[]{:S(2)}, u32[]{:S(2)}) async-start(bf16[16,2,24,384]{3,2,1,0:T(8,128)(2,1)} %broadcast_in_dim.5), calls=%async_computation.2 | async-start | bytes 1179648 | tf_op jit(solution)/shard_map/all_to_all | solution.py:150
  47.2 1.0 %copy-start.2 = (bf16[1,512,512]{2,1,0:T(8,128)(2,1)S(1)}, bf16[1,512,512]{2,1,0:T(8,128)(2,1)}, u32[]{:S(2)}) copy-start(bf16[1,512,512]{2,1,0:T(8,128)(2,1)} %param.5) | copy-start | bytes 1572868

commit v2 on v1

v2 whole, which is shorter than its diff:
```python
import numpy as np
import jax
import jax.numpy as jnp
from jax import lax
from jax.experimental import pallas as pl
from jax.experimental.pallas import tpu as pltpu
from jax.sharding import PartitionSpec as P

STEPS = 2
NP = 512
HALF = NP // 2
M = 384
REST = M - HALF
Y, Z, CORES = 8, 4, 2
PLANE = Y * CORES
CHUNK = M // PLANE


def make_tables():
    line = np.arange(NP)
    phases = (line[:, None] * line[None, :]) % NP
    angles = phases.astype(np.float32) * np.float32(2.0 * 3.141592653589793 / NP)
    cos_table, sin_table = np.cos(angles), np.sin(angles)
    tables = []
    for parity in (0, 1):
        cos_part = cos_table[parity::2, :HALF]
        sin_part = sin_table[parity::2, :HALF]
        tables.append(np.block([[cos_part, sin_part], [-sin_part, cos_part]]))
    tables = np.stack(tables).astype(jnp.bfloat16)
    return tables, np.ascontiguousarray(tables.transpose(0, 2, 1))


def matmul(left, right):
    return jnp.dot(left, right, preferred_element_type=jnp.float32)


def wide(values):
    return values.astype(jnp.float32)


def narrow(values):
    return values.astype(jnp.bfloat16)


def combine(left, right, parity):
    return left + right if parity == 0 else left - right


def pick(shares_ref, place_ref, step):
    total = None
    for place in range(shares_ref.shape[0]):
        share = shares_ref[place, step] if len(shares_ref.shape) == 4 else shares_ref[place]
        here = jnp.where(place_ref[step : step + 1] == place, 1.0, 0.0)
        total = wide(share) * here if total is None else total + wide(share) * here
    return narrow(total)


def pick_place_kernel(shares_ref, place_ref, out_ref):
    for step in range(STEPS):
        share = pick(shares_ref, place_ref, step)
        for receiver in range(out_ref.shape[0]):
            out_ref[receiver, step] = share


def pick_plane_kernel(shares_ref, place_ref, out_ref):
    for step in range(STEPS):
        share = pick(shares_ref, place_ref, step)
        for receiver in range(step, out_ref.shape[0], CORES):
            out_ref[receiver] = share


def side_by_side(left, col_parity):
    cols = slice(col_parity * HALF, (col_parity + 1) * HALF)
    return jnp.concatenate([jnp.concatenate([a[:HALF, cols], a[HALF:, cols]], axis=1) for a in left], axis=0)


def image_kernel(first_ref, second_ref, fwd_ref, inv_ref, spec_ref):
    quarters = []
    for field in (first_ref, second_ref):
        top_left, top_right = wide(field[:HALF, :HALF]), wide(field[:HALF, HALF:])
        low_left, low_right = wide(field[HALF:, :HALF]), wide(field[HALF:, HALF:])
        quarters.append((top_left, top_right, low_left, low_right))
    left = []
    for row_parity in (0, 1):
        folded = []
        for col_parity in (0, 1):
            parts = []
            for top_left, top_right, low_left, low_right in quarters:
                left_half = combine(top_left, low_left, row_parity)
                right_half = combine(top_right, low_right, row_parity)
                parts.append(narrow(combine(left_half, right_half, col_parity)))
            folded.append(jnp.concatenate(parts, axis=0))
        left.append(narrow(matmul(fwd_ref[row_parity], jnp.concatenate(folded, axis=1))))
    for col_parity in (0, 1):
        spec_ref[col_parity] = narrow(matmul(side_by_side(left, col_parity), inv_ref[col_parity]))


def correlate_kernel(shares_ref, spec_ref, fwd_ref, inv_ref, out_ref, field_ref, back_ref):
    for place in range(PLANE):
        field_ref[place * CHUNK : (place + 1) * CHUNK, :] = wide(shares_ref[place])
    left = []
    for row_parity in (0, 1):
        top = combine(field_ref[:REST], field_ref[HALF:], row_parity)
        rows = jnp.concatenate([top, field_ref[REST:HALF]], axis=0)
        folded = []
        for col_parity in (0, 1):
            first = combine(rows[:, :REST], rows[:, HALF:], col_parity)
            folded.append(narrow(jnp.concatenate([first, rows[:, REST:HALF]], axis=1)))
        left.append(narrow(matmul(fwd_ref[row_parity, :, :HALF], jnp.concatenate(folded, axis=1))))
    products = []
    for col_parity in (0, 1):
        tmpl = matmul(side_by_side(left, col_parity), inv_ref[col_parity])
        tmpl_re, tmpl_im = tmpl[:, :HALF], tmpl[:, HALF:]
        image_re, image_im = wide(spec_ref[col_parity, :, :HALF]), wide(spec_ref[col_parity, :, HALF:])
        prod_re = narrow(image_re * tmpl_re + image_im * tmpl_im)
        prod_im = narrow(image_im * tmpl_re - image_re * tmpl_im)
        products.append((prod_re, prod_im))
    left = []
    for row_parity in (0, 1):
        rows = slice(row_parity * HALF, (row_parity + 1) * HALF)
        stacked = [jnp.concatenate([prod_re[rows], prod_im[rows]], axis=0) for prod_re, prod_im in products]
        left.append(narrow(matmul(inv_ref[row_parity], jnp.concatenate(stacked, axis=1))))
    for col_parity in (0, 1):
        back_ref[col_parity] = matmul(side_by_side(left, col_parity), fwd_ref[col_parity])
    rows_out = out_ref.shape[1]
    groups = NP // rows_out
    for core in range(CORES):
        cols = slice(core * HALF, (core + 1) * HALF)
        for group in range(groups // 2):
            even = slice(group * rows_out, (group + 1) * rows_out)
            odd = slice(HALF + group * rows_out, HALF + (group + 1) * rows_out)
            even_even, even_odd = back_ref[0, even, cols], back_ref[1, even, cols]
            odd_even, odd_odd = back_ref[0, odd, cols], back_ref[1, odd, cols]
            even_left, odd_left = even_even + even_odd, odd_even + odd_odd
            even_right, odd_right = even_even - even_odd, odd_even - odd_odd
            upper = group * CORES + core
            lower = upper + groups // 2 * CORES
            out_ref[upper, :, :HALF] = narrow(even_left + odd_left)
            out_ref[upper, :, HALF:] = narrow(even_right + odd_right)
            out_ref[lower, :, :HALF] = narrow(even_left - odd_left)
            out_ref[lower, :, HALF:] = narrow(even_right - odd_right)


def pairwise(op, values):
    while len(values) > 1:
        values = [op(*values[i : i + 2]) for i in range(0, len(values), 2)]
    return values[0]


def statistics_kernel(values_ref, total_ref, squares_ref, largest_ref):
    scale = 1.0 / (NP * NP)
    count, height, width = values_ref.shape
    for row in range(0, height, 16):
        for col in range(0, width, 128):
            rows, cols = slice(row, row + 16), slice(col, col + 128)
            values = [wide(values_ref[template, rows, cols]) for template in range(count)]
            total_ref[0, rows, cols] = pairwise(jnp.add, values) * jnp.float32(scale)
            squares_ref[0, rows, cols] = pairwise(jnp.add, [v * v for v in values]) * jnp.float32(scale * scale)
            largest_ref[0, rows, cols] = pairwise(jnp.maximum, values) * jnp.float32(scale)


def call(kernel, name, outs, scratch, *operands):
    whole = pl.BlockSpec(memory_space=pltpu.VMEM)
    return pl.pallas_call(
        kernel,
        name=name,
        out_shape=outs,
        in_specs=[whole] * len(operands),
        out_specs=jax.tree.map(lambda _: whole, outs),
        scratch_shapes=scratch,
        compiler_params=pltpu.CompilerParams(vmem_limit_bytes=32 * 1024 * 1024),
    )(*operands)


def receive_template(own_template, owners):
    planes = [[(y * Z + z) * CORES + c for y in range(Y) for c in range(CORES)] for z in range(Z)]
    columns = [[(y * Z + z) * CORES + c for z in range(Z)] for y in range(Y) for c in range(CORES)]
    owner_z = owners // CORES % Z
    owner_place = owners // (Z * CORES) * CORES + owners % CORES
    owner_z, owner_place = (jnp.broadcast_to(place[:, None], (STEPS, M)) for place in (owner_z, owner_place))
    shares = own_template.reshape(PLANE, CHUNK, M)
    shares = lax.all_to_all(shares, "tile", 0, 0, axis_index_groups=planes)
    spread = jax.ShapeDtypeStruct((Z, STEPS, CHUNK, M), jnp.bfloat16)
    shares = call(pick_place_kernel, "pick_place", spread, [], shares, owner_place)
    shares = lax.all_to_all(shares, "tile", 0, 0, axis_index_groups=columns)
    spread = jax.ShapeDtypeStruct((PLANE, CHUNK, M), jnp.bfloat16)
    shares = call(pick_plane_kernel, "pick_plane", spread, [], shares, owner_z)
    return lax.all_to_all(shares, "tile", 0, 0, axis_index_groups=planes)


def image_fields(own_tile):
    tiles = lax.axis_size("tile")
    is_first = lax.axis_index("tile") % CORES == 0
    other_tile = lax.ppermute(own_tile, "tile", [(tile, tile ^ 1) for tile in range(tiles)])
    return jnp.where(is_first, own_tile, other_tile), jnp.where(is_first, other_tile, own_tile)


def per_device(image_tiles, templates, owners):
    fwd, inv = (jnp.asarray(table) for table in make_tables())
    groups_here = lax.axis_size("orient")
    tiles = lax.axis_size("tile")
    rows_out = NP // groups_here
    spectrum = (2, NP, NP)
    fields = image_fields(image_tiles[0])
    spec = call(image_kernel, "image_spectrum", jax.ShapeDtypeStruct(spectrum, jnp.bfloat16), [], *fields, fwd, inv)
    shares = receive_template(templates[0, 0], owners[0])
    values = call(
        correlate_kernel,
        "correlate",
        jax.ShapeDtypeStruct((groups_here * CORES, rows_out, NP), jnp.bfloat16),
        [pltpu.VMEM((M, M), jnp.float32), pltpu.VMEM(spectrum, jnp.float32)],
        shares,
        spec,
        fwd,
        inv,
    )
    across = [
        [group * tiles + pair * CORES + c for group in range(groups_here) for c in range(CORES)]
        for pair in range(tiles // CORES)
    ]
    values = lax.all_to_all(values, ("orient", "tile"), 0, 0, axis_index_groups=across)
    out = jax.ShapeDtypeStruct((1, rows_out, NP), jnp.float32)
    return call(statistics_kernel, "statistics", (out, out, out), [], values)


def solution(mesh):
    placed = (P("tile", None, None), P("orient", "tile", None, None), P("orient", None))
    return jax.shard_map(
        per_device,
        mesh=mesh,
        in_specs=placed,
        out_specs=(P("tile", "orient", None), P("tile", "orient", None), P("tile", "orient", None)),
        check_vma=False,
    )
```

time: 92.6 us -> 82.3 us (0.89)
  blocking collectives: 19.4 us -> 36.2 us
  waiting for transfers between devices: 28.9 us -> 19.9 us
  between operations: 8.29 us -> 0.72 us
  starting transfers between devices: 24.2 us -> 17.8 us
  Pallas kernels: 7.99 us -> 5.6 us
  local copies, waits for them, and re-layouts: 3.19 us -> 1.58 us
    all_to_all x1 -> x2, blocking collectives: 19.4 us -> 36.2 us  [the longest x1 19.8 us: per_device(): lax.all_to_all(values, ('orient', 'tile'), 0, 0, axis_index_groups=across)]
    all_to_all x3 -> x2, waiting for transfers between devices: 28.9 us -> 19.9 us  [the longest x1 10.3 us: receive_template(): shares = lax.all_to_all(shares, 'tile', 0, 0, axis_index_groups=planes)]
    all_to_all x3 -> x2, starting transfers between devices: 24.2 us -> 15.7 us  [the longest x1 10.3 us: receive_template(): shares = lax.all_to_all(shares, 'tile', 0, 0, axis_index_groups=planes)]
    pallas_call x3 -> x5, Pallas kernels: 7.99 us -> 5.6 us  [call(): pl.pallas_call(kernel, name=name, out_shape=outs, in_specs=[whole] * len(...]
    ppermute x0 -> x1, starting transfers between devices: none -> 2.13 us  [image_fields(): lax.ppermute(own_tile, 'tile', [(tile, tile ^ 1) for tile in range(tiles)])]
    broadcast_in_dim x2, local copies, waits for them, and re-layouts: 1.54 us -> 0.14 us  [receive_template(): jnp.broadcast_to(place[:, None], (STEPS, M))]
  transfers between devices with their start and end apart: 3 -> 3, of which waited for: 3 -> 2; matrix products, arithmetic and copies ran while one was open for 1% -> 0% of each run, Pallas kernels for 1% -> 3%
where the time goes in v2:
time: 82.3 us; the launch traced here: 81.9 us
  blocking collectives  36.2 us (44%)
  waiting for transfers between devices  19.9 us (24%)
  starting transfers between devices  17.8 us (22%)
  Pallas kernels  5.6 us (7%)
  local copies, waits for them, and re-layouts  1.58 us (2%)
    all_to_all x1, blocking collectives, per_device(): lax.all_to_all(values, ('orient', 'tile'), 0, 0, axis_index_groups=across)  19.8 us
    all_to_all x1, blocking collectives, receive_template(): shares = lax.all_to_all(shares, 'tile', 0, 0, axis_index_groups=columns)  16.4 us
    all_to_all x1, starting transfers between devices, receive_template(): shares = lax.all_to_all(shares, 'tile', 0, 0, axis_index_groups=planes)  10.3 us
    all_to_all x1, waiting for transfers between devices, receive_template(): shares = lax.all_to_all(shares, 'tile', 0, 0, axis_index_groups=planes)  10.3 us
    all_to_all x1, waiting for transfers between devices, receive_template(): return lax.all_to_all(shares, 'tile', 0, 0, axis_index_groups=planes)  9.58 us
    pallas_call x5, Pallas kernels, call(): pl.pallas_call(kernel, name=name, out_shape=outs, in_specs=[whole] * len(...  5.6 us
    all_to_all x1, starting transfers between devices, receive_template(): return lax.all_to_all(shares, 'tile', 0, 0, axis_index_groups=planes)  5.36 us
    ppermute x1, starting transfers between devices, image_fields(): lax.ppermute(own_tile, 'tile', [(tile, tile ^ 1) for tile in range(tiles)])  2.13 us
  transfers between devices with their start and end apart: 3, of which 2 were waited for; matrix products, arithmetic and copies ran while one was open for 0% of the time, Pallas kernels for 3%

profile of v2, /device:TPU:1, one launch (start us, length us, event | category | flops | bytes accessed | tf_op | source)
XLA Modules:
  0.0 81.9 jit_solution(6080657719268244617)
XLA Ops:
  0.6 0.0 copy-start.2
  0.6 10.3 %all-to-all-start = ((bf16[16,24,384]{2,1,0:T(8,128)(2,1)}), bf16[16,24,384]{2,1,0:T(8,128)(2,1)S(1)}, u32[]{:S(2)}, u32[]{:S(2)}) async-start(bf16[16,24,384]{2,1,0:T(8,128)(2,1)} %bitcast.29), calls=%async_computation | async-start | bytes 589824 | tf_op jit(solution)/shard_map/all_to_all | solution.py:182
  11.0 0.0 copy-start.3
  11.0 0.0 copy-done.2
  11.0 2.1 %collective-permute-start = (bf16[512,512]{1,0:T(8,128)(2,1)S(1)}, bf16[512,512]{1,0:T(8,128)(2,1)S(1)}, u32[]{:S(2)}, u32[]{:S(2)}) collective-permute-start(bf16[512,512]{1,0:T(8,128)(2,1)S(1)} %bitcast.28), channel_id=1, source_target_pairs={{0,1},{1,0},{2,3},{3,2},{4,5},{5,4},{6,7},{7,6},{8,9},{9,8},{10,11... | collective-permute-start | bytes 1572872 | tf_op jit(solution)/shard_map/ppermute | solution.py:194
  13.1 0.0 copy-done.3
  13.2 10.3 %all-to-all-done.shares_ref = bf16[16,24,384]{2,1,0:T(8,128)(2,1)S(1)} async-done(((bf16[16,24,384]{2,1,0:T(8,128)(2,1)}), bf16[16,24,384]{2,1,0:T(8,128)(2,1)S(1)}, u32[]{:S(2)}, u32[]{:S(2)}) %all-to-all-start) | async-done | bytes 294944 | tf_op jit(solution)/shard_map/all_to_all | solution.py:182
  23.5 0.1 broadcast_in_dim.4.place_ref
  23.5 0.1 pick_place.1
  23.7 16.4 %all_to_all.20.shares_ref = bf16[4,2,24,384]{3,2,1,0:T(8,128)(2,1)S(1)} all-to-all(bf16[4,2,24,384]{3,2,1,0:T(8,128)(2,1)S(1)} %pick_place.1), channel_id=1, replica_groups={{0,2,4,6},{1,3,5,7},{8,10,12,14},{9,11,13,15},{16,18,20,22},{17,19,21,2..., dimensions={0} | all-to-all | bytes 294912 | tf_op jit(solution)/shard_map/all_to_all | solution.py:185
  40.1 0.1 broadcast_in_dim.5.place_ref
  40.2 0.8 pick_plane.1
  40.9 5.4 %all-to-all-start.2 = ((bf16[16,24,384]{2,1,0:T(8,128)(2,1)}), bf16[16,24,384]{2,1,0:T(8,128)(2,1)S(1)}, u32[]{:S(2)}, u32[]{:S(2)}) async-start(bf16[16,24,384]{2,1,0:T(8,128)(2,1)} %pick_plane.1), calls=%async_computation.2 | async-start | bytes 589824 | tf_op jit(solution)/shard_map/all_to_all | solution.py:188
  46.3 0.0 copy-start
  46.3 0.0 copy-start.1
  46.3 0.0 collective-permute-done
  46.3 0.1 broadcast_select_fusion
  46.4 1.1 %copy-done = bf16[2,512,512]{2,1,0:T(8,128)(2,1)S(1)} copy-done((bf16[2,512,512]{2,1,0:T(8,128)(2,1)S(1)}, bf16[2,512,512]{2,1,0:T(8,128)(2,1)}, u32[]{:S(2)}) %copy-start) | copy-done | bytes 1048600
  47.5 0.3 copy-done.1
  47.8 1.3 %image_spectrum.1.spec_ref = bf16[2,512,512]{2,1,0:T(8,128)(2,1)S(1)} custom-call(bf16[512,512]{1,0:T(8,128)(2,1)S(1)} %get-tuple-element.4.first_ref, bf16[512,512]{1,0:T(8,128)(2,1)S(1)} %get-tuple-element.3.second_ref, bf16[2,512,512]{2,1,0:T(8,128)(2,1)S(1)} %copy-done.1, bf16[2,512,512]{2,1,0:T(8,128)(2,1)S(1)} %copy-done), custom_call_target="tpu_custom_call" | custom-call | tf_op jit(solution)/shard_map/image_spectrum/pallas_call | solution.py:164
  49.2 9.6 %all-to-all-done.2.shares_ref = bf16[16,24,384]{2,1,0:T(8,128)(2,1)S(1)} async-done(((bf16[16,24,384]{2,1,0:T(8,128)(2,1)}), bf16[16,24,384]{2,1,0:T(8,128)(2,1)S(1)}, u32[]{:S(2)}, u32[]{:S(2)}) %all-to-all-start.2) | async-done | bytes 294944 | tf_op jit(solution)/shard_map/all_to_all | solution.py:188
  58.7 2.3 %correlate.1 = bf16[16,64,512]{2,1,0:T(8,128)(2,1)S(1)} custom-call(bf16[16,24,384]{2,1,0:T(8,128)(2,1)S(1)} %all-to-all-done.2.shares_ref, bf16[2,512,512]{2,1,0:T(8,128)(2,1)S(1)} %image_spectrum.1.spec_ref, bf16[2,512,512]{2,1,0:T(8,128)(2,1)S(1)} %copy-done.1, bf16[2,512,512]{2,1,0:T(8,128)(2,1)S(1)} %copy-done), custom_call_target="tpu_custom_call" | custom-call | tf_op jit(solution)/shard_map/correlate/pallas_call | solution.py:164
  61.1 19.8 %all_to_all.21.values_ref = bf16[16,64,512]{2,1,0:T(8,128)(2,1)S(1)} all-to-all(bf16[16,64,512]{2,1,0:T(8,128)(2,1)S(1)} %correlate.1), channel_id=1, replica_groups={{0,1,64,65,128,129,192,193,256,257,320,321,384,385,448,449},{2,3,66,67,..., dimensions={0} | all-to-all | bytes 2097152 | tf_op jit(solution)/shard_map/all_to_all | solution.py:221
  80.8 1.0 %statistics.1 = (f32[1,64,512]{2,1,0:T(8,128)}, f32[1,64,512]{2,1,0:T(8,128)}, f32[1,64,512]{2,1,0:T(8,128)}) custom-call(bf16[16,64,512]{2,1,0:T(8,128)(2,1)S(1)} %all_to_all.21.values_ref), custom_call_target="tpu_custom_call" | custom-call | tf_op jit(solution)/shard_map/statistics/pallas_call | solution.py:164
  (1 shorter events, 0.0 us)
Async XLA Ops:
  0.6 10.4 %copy-start.2 = (bf16[1,512,512]{2,1,0:T(8,128)(2,1)S(1)}, bf16[1,512,512]{2,1,0:T(8,128)(2,1)}, u32[]{:S(2)}) copy-start(bf16[1,512,512]{2,1,0:T(8,128)(2,1)} %param.5) | copy-start | bytes 1572868
  0.6 22.8 %all-to-all-start = ((bf16[16,24,384]{2,1,0:T(8,128)(2,1)}), bf16[16,24,384]{2,1,0:T(8,128)(2,1)S(1)}, u32[]{:S(2)}, u32[]{:S(2)}) async-start(bf16[16,24,384]{2,1,0:T(8,128)(2,1)} %bitcast.29), calls=%async_computation | async-start | bytes 589824 | tf_op jit(solution)/shard_map/all_to_all | solution.py:182
  11.0 2.2 %copy-start.3 = (s32[1,2]{1,0:T(1,128)S(1)}, s32[1,2]{1,0:T(1,128)}, u32[]{:S(2)}) copy-start(s32[1,2]{1,0:T(1,128)} %param.7) | copy-start | bytes 28
  11.0 35.3 %collective-permute-start = (bf16[512,512]{1,0:T(8,128)(2,1)S(1)}, bf16[512,512]{1,0:T(8,128)(2,1)S(1)}, u32[]{:S(2)}, u32[]{:S(2)}) collective-permute-start(bf16[512,512]{1,0:T(8,128)(2,1)S(1)} %bitcast.28), channel_id=1, source_target_pairs={{0,1},{1,0},{2,3},{3,2},{4,5},{5,4},{6,7},{7,6},{8,9},{9,8},{10,11... | collective-permute-start | bytes 1572872 | tf_op jit(solution)/shard_map/ppermute | solution.py:194
  40.9 17.8 %all-to-all-start.2 = ((bf16[16,24,384]{2,1,0:T(8,128)(2,1)}), bf16[16,24,384]{2,1,0:T(8,128)(2,1)S(1)}, u32[]{:S(2)}, u32[]{:S(2)}) async-start(bf16[16,24,384]{2,1,0:T(8,128)(2,1)} %pick_plane.1), calls=%async_computation.2 | async-start | bytes 589824 | tf_op jit(solution)/shard_map/all_to_all | solution.py:188
  46.3 1.2 %copy-start = (bf16[2,512,512]{2,1,0:T(8,128)(2,1)S(1)}, bf16[2,512,512]{2,1,0:T(8,128)(2,1)}, u32[]{:S(2)}) copy-start(bf16[2,512,512]{2,1,0:T(8,128)(2,1)} %constant.64.clone.inv_ref) | copy-start | bytes 3145732
  46.3 1.5 %copy-start.1 = (bf16[2,512,512]{2,1,0:T(8,128)(2,1)S(1)}, bf16[2,512,512]{2,1,0:T(8,128)(2,1)}, u32[]{:S(2)}) copy-start(bf16[2,512,512]{2,1,0:T(8,128)(2,1)} %constant.63.clone.fwd_ref) | copy-start | bytes 3145732

commit v3 on v2

--- a/solution.py
+++ b/solution.py
@@ -65,8 +65,8 @@
 def pick_plane_kernel(shares_ref, place_ref, out_ref):
     for step in range(STEPS):
         share = pick(shares_ref, place_ref, step)
-        for receiver in range(step, out_ref.shape[0], CORES):
-            out_ref[receiver] = share
+        for y in range(Y):
+            out_ref[plane_place(y, step)] = share
 
 
 def side_by_side(left, col_parity):
@@ -124,6 +124,7 @@
         back_ref[col_parity] = matmul(side_by_side(left, col_parity), fwd_ref[col_parity])
     rows_out = out_ref.shape[1]
     groups = NP // rows_out
+    members = result_members()
     for core in range(CORES):
         cols = slice(core * HALF, (core + 1) * HALF)
         for group in range(groups // 2):
@@ -133,8 +134,8 @@
             odd_even, odd_odd = back_ref[0, odd, cols], back_ref[1, odd, cols]
             even_left, odd_left = even_even + even_odd, odd_even + odd_odd
             even_right, odd_right = even_even - even_odd, odd_even - odd_odd
-            upper = group * CORES + core
-            lower = upper + groups // 2 * CORES
+            upper = members.index((group, core))
+            lower = members.index((group + groups // 2, core))
             out_ref[upper, :, :HALF] = narrow(even_left + odd_left)
             out_ref[upper, :, HALF:] = narrow(even_right + odd_right)
             out_ref[lower, :, :HALF] = narrow(even_left - odd_left)
@@ -172,11 +173,24 @@
     )(*operands)
 
 
+def plane_place(y, core):
+    return (3 * y + 4) % Y * CORES + core
+
+
+def column_place(z):
+    return (z + 2) % Z
+
+
+def result_members():
+    return [(zl * 4 + (x + 2) % 4, c) for zl in range(2) for x in range(4) for c in range(CORES)]
+
+
 def receive_template(own_template, owners):
-    planes = [[(y * Z + z) * CORES + c for y in range(Y) for c in range(CORES)] for z in range(Z)]
-    columns = [[(y * Z + z) * CORES + c for z in range(Z)] for y in range(Y) for c in range(CORES)]
-    owner_z = owners // CORES % Z
-    owner_place = owners // (Z * CORES) * CORES + owners % CORES
+    plane_members = sorted(((y, c) for y in range(Y) for c in range(CORES)), key=lambda member: plane_place(*member))
+    planes = [[(y * Z + z) * CORES + c for y, c in plane_members] for z in range(Z)]
+    columns = [[(y * Z + z) * CORES + c for z in sorted(range(Z), key=column_place)] for y in range(Y) for c in range(CORES)]
+    owner_z = column_place(owners // CORES % Z)
+    owner_place = plane_place(owners // (Z * CORES), owners % CORES)
     owner_z, owner_place = (jnp.broadcast_to(place[:, None], (STEPS, M)) for place in (owner_z, owner_place))
     shares = own_template.reshape(PLANE, CHUNK, M)
     shares = lax.all_to_all(shares, "tile", 0, 0, axis_index_groups=planes)
@@ -214,10 +228,7 @@
         fwd,
         inv,
     )
-    across = [
-        [group * tiles + pair * CORES + c for group in range(groups_here) for c in range(CORES)]
-        for pair in range(tiles // CORES)
-    ]
+    across = [[group * tiles + pair * CORES + c for group, c in result_members()] for pair in range(tiles // CORES)]
     values = lax.all_to_all(values, ("orient", "tile"), 0, 0, axis_index_groups=across)
     out = jax.ShapeDtypeStruct((1, rows_out, NP), jnp.float32)
     return call(statistics_kernel, "statistics", (out, out, out), [], values)

time: 82.3 us -> 75.1 us (0.913)
  waiting for transfers between devices: 19.9 us -> 10.1 us
  starting transfers between devices: 17.8 us -> 24.6 us
  blocking collectives: 36.2 us -> 32 us
    all_to_all x1, waiting for transfers between devices: 10.3 us -> 5.3 us  [receive_template(): shares = lax.all_to_all(shares, 'tile', 0, 0, axis_index_groups=planes)]
    all_to_all x1, waiting for transfers between devices: 9.58 us -> 4.75 us  [receive_template(): return lax.all_to_all(shares, 'tile', 0, 0, axis_index_groups=planes)]
    all_to_all x1, blocking collectives: 16.4 us -> 12.7 us  [receive_template(): shares = lax.all_to_all(shares, 'tile', 0, 0, axis_index_groups=columns)]
    all_to_all x1, starting transfers between devices: 10.3 us -> 13.9 us  [receive_template(): shares = lax.all_to_all(shares, 'tile', 0, 0, axis_index_groups=planes)]
    all_to_all x1, starting transfers between devices: 5.36 us -> 8.49 us  [receive_template(): return lax.all_to_all(shares, 'tile', 0, 0, axis_index_groups=planes)]
where the time goes in v3:
time: 75.1 us; the launch traced here: 74.7 us
  blocking collectives  32 us (43%)
  starting transfers between devices  24.6 us (33%)
  waiting for transfers between devices  10.1 us (13%)
  Pallas kernels  5.6 us (7%)
  local copies, waits for them, and re-layouts  1.58 us (2%)
    all_to_all x1, blocking collectives, per_device(): lax.all_to_all(values, ('orient', 'tile'), 0, 0, axis_index_groups=across)  19.3 us
    all_to_all x1, starting transfers between devices, receive_template(): shares = lax.all_to_all(shares, 'tile', 0, 0, axis_index_groups=planes)  13.9 us
    all_to_all x1, blocking collectives, receive_template(): shares = lax.all_to_all(shares, 'tile', 0, 0, axis_index_groups=columns)  12.7 us
    all_to_all x1, starting transfers between devices, receive_template(): return lax.all_to_all(shares, 'tile', 0, 0, axis_index_groups=planes)  8.49 us
    pallas_call x5, Pallas kernels, call(): pl.pallas_call(kernel, name=name, out_shape=outs, in_specs=[whole] * len(...  5.6 us
    all_to_all x1, waiting for transfers between devices, receive_template(): shares = lax.all_to_all(shares, 'tile', 0, 0, axis_index_groups=planes)  5.3 us
    all_to_all x1, waiting for transfers between devices, receive_template(): return lax.all_to_all(shares, 'tile', 0, 0, axis_index_groups=planes)  4.75 us
    ppermute x1, starting transfers between devices, image_fields(): lax.ppermute(own_tile, 'tile', [(tile, tile ^ 1) for tile in range(tiles)])  2.27 us
  transfers between devices with their start and end apart: 3, of which 2 were waited for; matrix products, arithmetic and copies ran while one was open for 0% of the time, Pallas kernels for 3%

profile of v3, /device:TPU:1, one launch (start us, length us, event | category | flops | bytes accessed | tf_op | source)
XLA Modules:
  0.0 74.7 jit_solution(9465158346721582893)
XLA Ops:
  0.6 0.0 copy-start.2
  0.6 13.9 %all-to-all-start = ((bf16[16,24,384]{2,1,0:T(8,128)(2,1)}), bf16[16,24,384]{2,1,0:T(8,128)(2,1)S(1)}, u32[]{:S(2)}, u32[]{:S(2)}) async-start(bf16[16,24,384]{2,1,0:T(8,128)(2,1)} %bitcast.29), calls=%async_computation | async-start | bytes 589824 | tf_op jit(solution)/shard_map/all_to_all | solution.py:196
  14.5 0.0 copy-start.3
  14.5 0.0 copy-done.2
  14.5 2.3 %collective-permute-start = (bf16[512,512]{1,0:T(8,128)(2,1)S(1)}, bf16[512,512]{1,0:T(8,128)(2,1)S(1)}, u32[]{:S(2)}, u32[]{:S(2)}) collective-permute-start(bf16[512,512]{1,0:T(8,128)(2,1)S(1)} %bitcast.28), channel_id=1, source_target_pairs={{0,1},{1,0},{2,3},{3,2},{4,5},{5,4},{6,7},{7,6},{8,9},{9,8},{10,11... | collective-permute-start | bytes 1572872 | tf_op jit(solution)/shard_map/ppermute | solution.py:208
  16.8 0.0 copy-done.3
  16.9 5.3 %all-to-all-done.shares_ref = bf16[16,24,384]{2,1,0:T(8,128)(2,1)S(1)} async-done(((bf16[16,24,384]{2,1,0:T(8,128)(2,1)}), bf16[16,24,384]{2,1,0:T(8,128)(2,1)S(1)}, u32[]{:S(2)}, u32[]{:S(2)}) %all-to-all-start) | async-done | bytes 294944 | tf_op jit(solution)/shard_map/all_to_all | solution.py:196
  22.2 0.1 broadcast_in_dim.4.place_ref
  22.2 0.1 pick_place.1
  22.4 12.7 %all_to_all.20.shares_ref = bf16[4,2,24,384]{3,2,1,0:T(8,128)(2,1)S(1)} all-to-all(bf16[4,2,24,384]{3,2,1,0:T(8,128)(2,1)S(1)} %pick_place.1), channel_id=1, replica_groups={{4,6,0,2},{5,7,1,3},{12,14,8,10},{13,15,9,11},{20,22,16,18},{21,23,17,1..., dimensions={0} | all-to-all | bytes 294912 | tf_op jit(solution)/shard_map/all_to_all | solution.py:199
  35.1 0.1 broadcast_in_dim.5.place_ref
  35.2 0.8 %pick_plane.1 = bf16[16,24,384]{2,1,0:T(8,128)(2,1)} custom-call(bf16[4,2,24,384]{3,2,1,0:T(8,128)(2,1)S(1)} %all_to_all.20.shares_ref, s32[2,384]{1,0:T(2,128)S(1)} %broadcast_in_dim.5.place_ref), custom_call_target="tpu_custom_call" | custom-call | tf_op jit(solution)/shard_map/pick_plane/pallas_call | solution.py:165
  35.9 8.5 %all-to-all-start.2 = ((bf16[16,24,384]{2,1,0:T(8,128)(2,1)}), bf16[16,24,384]{2,1,0:T(8,128)(2,1)S(1)}, u32[]{:S(2)}, u32[]{:S(2)}) async-start(bf16[16,24,384]{2,1,0:T(8,128)(2,1)} %pick_plane.1), calls=%async_computation.2 | async-start | bytes 589824 | tf_op jit(solution)/shard_map/all_to_all | solution.py:202
  44.4 0.0 copy-start
  44.4 0.0 copy-start.1
  44.5 0.0 collective-permute-done
  44.5 0.1 broadcast_select_fusion
  44.6 1.1 %copy-done = bf16[2,512,512]{2,1,0:T(8,128)(2,1)S(1)} copy-done((bf16[2,512,512]{2,1,0:T(8,128)(2,1)S(1)}, bf16[2,512,512]{2,1,0:T(8,128)(2,1)}, u32[]{:S(2)}) %copy-start) | copy-done | bytes 1048600
  45.7 0.3 copy-done.1
  46.0 1.3 %image_spectrum.1.spec_ref = bf16[2,512,512]{2,1,0:T(8,128)(2,1)S(1)} custom-call(bf16[512,512]{1,0:T(8,128)(2,1)S(1)} %get-tuple-element.4.first_ref, bf16[512,512]{1,0:T(8,128)(2,1)S(1)} %get-tuple-element.3.second_ref, bf16[2,512,512]{2,1,0:T(8,128)(2,1)S(1)} %copy-done.1, bf16[2,512,512]{2,1,0:T(8,128)(2,1)S(1)} %copy-done), custom_call_target="tpu_custom_call" | custom-call | tf_op jit(solution)/shard_map/image_spectrum/pallas_call | solution.py:165
  47.3 4.8 %all-to-all-done.2.shares_ref = bf16[16,24,384]{2,1,0:T(8,128)(2,1)S(1)} async-done(((bf16[16,24,384]{2,1,0:T(8,128)(2,1)}), bf16[16,24,384]{2,1,0:T(8,128)(2,1)S(1)}, u32[]{:S(2)}, u32[]{:S(2)}) %all-to-all-start.2) | async-done | bytes 294944 | tf_op jit(solution)/shard_map/all_to_all | solution.py:202
  52.1 2.3 %correlate.1 = bf16[16,64,512]{2,1,0:T(8,128)(2,1)S(1)} custom-call(bf16[16,24,384]{2,1,0:T(8,128)(2,1)S(1)} %all-to-all-done.2.shares_ref, bf16[2,512,512]{2,1,0:T(8,128)(2,1)S(1)} %image_spectrum.1.spec_ref, bf16[2,512,512]{2,1,0:T(8,128)(2,1)S(1)} %copy-done.1, bf16[2,512,512]{2,1,0:T(8,128)(2,1)S(1)} %copy-done), custom_call_target="tpu_custom_call" | custom-call | tf_op jit(solution)/shard_map/correlate/pallas_call | solution.py:165
  54.4 19.3 %all_to_all.21.values_ref = bf16[16,64,512]{2,1,0:T(8,128)(2,1)S(1)} all-to-all(bf16[16,64,512]{2,1,0:T(8,128)(2,1)S(1)} %correlate.1), channel_id=1, replica_groups={{128,129,192,193,0,1,64,65,384,385,448,449,256,257,320,321},{130,131,19..., dimensions={0} | all-to-all | bytes 2097152 | tf_op jit(solution)/shard_map/all_to_all | solution.py:232
  73.7 1.0 %statistics.1 = (f32[1,64,512]{2,1,0:T(8,128)}, f32[1,64,512]{2,1,0:T(8,128)}, f32[1,64,512]{2,1,0:T(8,128)}) custom-call(bf16[16,64,512]{2,1,0:T(8,128)(2,1)S(1)} %all_to_all.21.values_ref), custom_call_target="tpu_custom_call" | custom-call | tf_op jit(solution)/shard_map/statistics/pallas_call | solution.py:165
  (1 shorter events, 0.0 us)
Async XLA Ops:
  0.6 13.9 %copy-start.2 = (bf16[1,512,512]{2,1,0:T(8,128)(2,1)S(1)}, bf16[1,512,512]{2,1,0:T(8,128)(2,1)}, u32[]{:S(2)}) copy-start(bf16[1,512,512]{2,1,0:T(8,128)(2,1)} %param.5) | copy-start | bytes 1572868
  0.6 21.5 %all-to-all-start = ((bf16[16,24,384]{2,1,0:T(8,128)(2,1)}), bf16[16,24,384]{2,1,0:T(8,128)(2,1)S(1)}, u32[]{:S(2)}, u32[]{:S(2)}) async-start(bf16[16,24,384]{2,1,0:T(8,128)(2,1)} %bitcast.29), calls=%async_computation | async-start | bytes 589824 | tf_op jit(solution)/shard_map/all_to_all | solution.py:196
  14.5 2.3 %copy-start.3 = (s32[1,2]{1,0:T(1,128)S(1)}, s32[1,2]{1,0:T(1,128)}, u32[]{:S(2)}) copy-start(s32[1,2]{1,0:T(1,128)} %param.7) | copy-start | bytes 28
  14.5 29.9 %collective-permute-start = (bf16[512,512]{1,0:T(8,128)(2,1)S(1)}, bf16[512,512]{1,0:T(8,128)(2,1)S(1)}, u32[]{:S(2)}, u32[]{:S(2)}) collective-permute-start(bf16[512,512]{1,0:T(8,128)(2,1)S(1)} %bitcast.28), channel_id=1, source_target_pairs={{0,1},{1,0},{2,3},{3,2},{4,5},{5,4},{6,7},{7,6},{8,9},{9,8},{10,11... | collective-permute-start | bytes 1572872 | tf_op jit(solution)/shard_map/ppermute | solution.py:208
  35.9 16.1 %all-to-all-start.2 = ((bf16[16,24,384]{2,1,0:T(8,128)(2,1)}), bf16[16,24,384]{2,1,0:T(8,128)(2,1)S(1)}, u32[]{:S(2)}, u32[]{:S(2)}) async-start(bf16[16,24,384]{2,1,0:T(8,128)(2,1)} %pick_plane.1), calls=%async_computation.2 | async-start | bytes 589824 | tf_op jit(solution)/shard_map/all_to_all | solution.py:202
  44.4 1.2 %copy-start = (bf16[2,512,512]{2,1,0:T(8,128)(2,1)S(1)}, bf16[2,512,512]{2,1,0:T(8,128)(2,1)}, u32[]{:S(2)}) copy-start(bf16[2,512,512]{2,1,0:T(8,128)(2,1)} %constant.80.clone.inv_ref) | copy-start | bytes 3145732
  44.4 1.5 %copy-start.1 = (bf16[2,512,512]{2,1,0:T(8,128)(2,1)S(1)}, bf16[2,512,512]{2,1,0:T(8,128)(2,1)}, u32[]{:S(2)}) copy-start(bf16[2,512,512]{2,1,0:T(8,128)(2,1)} %constant.79.clone.fwd_ref) | copy-start | bytes 3145732

commit v4 on v3

--- a/solution.py
+++ b/solution.py
@@ -66,7 +66,7 @@
     for step in range(STEPS):
         share = pick(shares_ref, place_ref, step)
         for y in range(Y):
-            out_ref[plane_place(y, step)] = share
+            out_ref[gather_members().index((y, step))] = share
 
 
 def side_by_side(left, col_parity):
@@ -74,11 +74,11 @@
     return jnp.concatenate([jnp.concatenate([a[:HALF, cols], a[HALF:, cols]], axis=1) for a in left], axis=0)
 
 
-def image_kernel(first_ref, second_ref, fwd_ref, inv_ref, spec_ref):
+def image_kernel(top_ref, low_ref, fwd_ref, inv_ref, spec_ref):
     quarters = []
-    for field in (first_ref, second_ref):
-        top_left, top_right = wide(field[:HALF, :HALF]), wide(field[:HALF, HALF:])
-        low_left, low_right = wide(field[HALF:, :HALF]), wide(field[HALF:, HALF:])
+    for core in range(CORES):
+        top_left, top_right = wide(top_ref[core, :, :HALF]), wide(top_ref[core, :, HALF:])
+        low_left, low_right = wide(low_ref[core, :, :HALF]), wide(low_ref[core, :, HALF:])
         quarters.append((top_left, top_right, low_left, low_right))
     left = []
     for row_parity in (0, 1):
@@ -96,8 +96,9 @@
 
 
 def correlate_kernel(shares_ref, spec_ref, fwd_ref, inv_ref, out_ref, field_ref, back_ref):
-    for place in range(PLANE):
-        field_ref[place * CHUNK : (place + 1) * CHUNK, :] = wide(shares_ref[place])
+    for source, member in enumerate(gather_members()):
+        place = plane_place(*member)
+        field_ref[place * CHUNK : (place + 1) * CHUNK, :] = wide(shares_ref[source])
     left = []
     for row_parity in (0, 1):
         top = combine(field_ref[:REST], field_ref[HALF:], row_parity)
@@ -177,36 +178,41 @@
     return (3 * y + 4) % Y * CORES + core
 
 
+def gather_members():
+    return sorted(((y, c) for y in range(Y) for c in range(CORES)), key=lambda member: plane_place(*member))
+
+
 def column_place(z):
     return (z + 2) % Z
 
 
 def result_members():
-    return [(zl * 4 + (x + 2) % 4, c) for zl in range(2) for x in range(4) for c in range(CORES)]
-
-
-def receive_template(own_template, owners):
+    return [(zl * 4 + (x + 2) % 4, c) for x in range(4) for c in range(CORES) for zl in range(2)]
+
+
+def receive_template(own_template, owners, spec):
     plane_members = sorted(((y, c) for y in range(Y) for c in range(CORES)), key=lambda member: plane_place(*member))
     planes = [[(y * Z + z) * CORES + c for y, c in plane_members] for z in range(Z)]
+    gather_planes = [[(y * Z + z) * CORES + c for y, c in gather_members()] for z in range(Z)]
     columns = [[(y * Z + z) * CORES + c for z in sorted(range(Z), key=column_place)] for y in range(Y) for c in range(CORES)]
     owner_z = column_place(owners // CORES % Z)
     owner_place = plane_place(owners // (Z * CORES), owners % CORES)
     owner_z, owner_place = (jnp.broadcast_to(place[:, None], (STEPS, M)) for place in (owner_z, owner_place))
     shares = own_template.reshape(PLANE, CHUNK, M)
     shares = lax.all_to_all(shares, "tile", 0, 0, axis_index_groups=planes)
+    shares, spec = lax.optimization_barrier((shares, spec))
     spread = jax.ShapeDtypeStruct((Z, STEPS, CHUNK, M), jnp.bfloat16)
     shares = call(pick_place_kernel, "pick_place", spread, [], shares, owner_place)
     shares = lax.all_to_all(shares, "tile", 0, 0, axis_index_groups=columns)
     spread = jax.ShapeDtypeStruct((PLANE, CHUNK, M), jnp.bfloat16)
     shares = call(pick_plane_kernel, "pick_plane", spread, [], shares, owner_z)
-    return lax.all_to_all(shares, "tile", 0, 0, axis_index_groups=planes)
+    return lax.all_to_all(shares, "tile", 0, 0, axis_index_groups=gather_planes), spec
 
 
 def image_fields(own_tile):
-    tiles = lax.axis_size("tile")
-    is_first = lax.axis_index("tile") % CORES == 0
-    other_tile = lax.ppermute(own_tile, "tile", [(tile, tile ^ 1) for tile in range(tiles)])
-    return jnp.where(is_first, own_tile, other_tile), jnp.where(is_first, other_tile, own_tile)
+    pairs = [[tile, tile + 1] for tile in range(0, lax.axis_size("tile"), CORES)]
+    halves = [lax.all_gather(half, "tile", axis_index_groups=pairs) for half in (own_tile[:HALF], own_tile[HALF:])]
+    return halves
 
 
 def per_device(image_tiles, templates, owners):
@@ -217,7 +223,7 @@
     spectrum = (2, NP, NP)
     fields = image_fields(image_tiles[0])
     spec = call(image_kernel, "image_spectrum", jax.ShapeDtypeStruct(spectrum, jnp.bfloat16), [], *fields, fwd, inv)
-    shares = receive_template(templates[0, 0], owners[0])
+    shares, spec = receive_template(templates[0, 0], owners[0], spec)
     values = call(
         correlate_kernel,
         "correlate",

time: 75.1 us -> 73.8 us (0.983)
  blocking collectives: 32 us -> 52.1 us
  starting transfers between devices: 24.6 us -> 13.9 us
  waiting for transfers between devices: 10.1 us -> 1.69 us
  local copies, waits for them, and re-layouts: 1.58 us -> 0.2 us
    all_to_all x0 -> x1, blocking collectives: none -> 15.9 us  [receive_template(): lax.all_to_all(shares, 'tile', 0, 0, axis_index_groups=gather_planes)]
    all_to_all x1 -> x0, starting transfers between devices: 8.49 us -> none  [receive_template(): return lax.all_to_all(shares, 'tile', 0, 0, axis_index_groups=planes)]
    all_to_all x1 -> x0, waiting for transfers between devices: 4.75 us -> none  [receive_template(): return lax.all_to_all(shares, 'tile', 0, 0, axis_index_groups=planes)]
    all_gather x0 -> x2, blocking collectives: none -> 4.48 us  [image_fields(): lax.all_gather(half, 'tile', axis_index_groups=pairs)]
    all_to_all x1, waiting for transfers between devices: 5.3 us -> 1.69 us  [receive_template(): shares = lax.all_to_all(shares, 'tile', 0, 0, axis_index_groups=planes)]
    ppermute x1 -> x0, starting transfers between devices: 2.27 us -> none  [image_fields(): lax.ppermute(own_tile, 'tile', [(tile, tile ^ 1) for tile in range(tiles)])]
    unnamed x8, local copies, waits for them, and re-layouts: 1.44 us -> 0.02 us
  transfers between devices with their start and end apart: 3 -> 1, of which waited for: 2 -> 1; matrix products, arithmetic and copies ran while one was open for 0% -> 0% of each run, Pallas kernels for 3% -> 2%
where the time goes in v4:
time: 73.8 us; the launch traced here: 73.5 us
  blocking collectives  52.1 us (71%)
  starting transfers between devices  13.9 us (19%)
  Pallas kernels  4.89 us (7%)
  waiting for transfers between devices  1.69 us (2%)
    all_to_all x1, blocking collectives, per_device(): lax.all_to_all(values, ('orient', 'tile'), 0, 0, axis_index_groups=across)  18.9 us
    all_to_all x1, blocking collectives, receive_template(): lax.all_to_all(shares, 'tile', 0, 0, axis_index_groups=gather_planes)  15.9 us
    all_to_all x1, starting transfers between devices, receive_template(): shares = lax.all_to_all(shares, 'tile', 0, 0, axis_index_groups=planes)  13.9 us
    all_to_all x1, blocking collectives, receive_template(): shares = lax.all_to_all(shares, 'tile', 0, 0, axis_index_groups=columns)  12.7 us
    pallas_call x5, Pallas kernels, call(): pl.pallas_call(kernel, name=name, out_shape=outs, in_specs=[whole] * len(...  4.89 us
    all_gather x2, blocking collectives, image_fields(): lax.all_gather(half, 'tile', axis_index_groups=pairs)  4.48 us
    all_to_all x1, waiting for transfers between devices, receive_template(): shares = lax.all_to_all(shares, 'tile', 0, 0, axis_index_groups=planes)  1.69 us
  transfers between devices with their start and end apart: 1, of which 1 were waited for; matrix products, arithmetic and copies ran while one was open for 0% of the time, Pallas kernels for 2%

profile of v4, /device:TPU:1, one launch (start us, length us, event | category | flops | bytes accessed | tf_op | source)
XLA Modules:
  0.0 73.5 jit_solution(6945507935497608467)
XLA Ops:
  0.6 0.0 copy-start.2
  0.6 13.9 %all-to-all-start = ((bf16[16,24,384]{2,1,0:T(8,128)(2,1)}), bf16[16,24,384]{2,1,0:T(8,128)(2,1)S(1)}, u32[]{:S(2)}, u32[]{:S(2)}) async-start(bf16[16,24,384]{2,1,0:T(8,128)(2,1)} %bitcast.25), calls=%async_computation | async-start | bytes 589824 | tf_op jit(solution)/shard_map/all_to_all | solution.py:202
  14.5 0.0 copy-done.2
  14.5 0.0 copy-start.1
  14.6 0.0 copy-start
  14.6 2.3 %all_gather.8.top_ref = bf16[2,256,512]{2,1,0:T(8,128)(2,1)S(1)} all-gather(bf16[1,256,512]{2,1,0:T(8,128)(2,1)S(1)} %get-tuple-element.8), channel_id=1, replica_groups={{0,1},{2,3},{4,5},{6,7},{8,9},{10,11},{12,13},{14,15},{16,17},{18,19},{..., dimensions={0}, use_global_device_ids=true | all-gather | bytes 786432 | tf_op jit(solution)/shard_map/all_gather | solution.py:214
  16.9 2.2 %all_gather.9.low_ref = bf16[2,256,512]{2,1,0:T(8,128)(2,1)S(1)} all-gather(bf16[1,256,512]{2,1,0:T(8,128)(2,1)S(1)} %get-tuple-element.7), channel_id=1, replica_groups={{0,1},{2,3},{4,5},{6,7},{8,9},{10,11},{12,13},{14,15},{16,17},{18,19},{..., dimensions={0}, use_global_device_ids=true | all-gather | bytes 786432 | tf_op jit(solution)/shard_map/all_gather | solution.py:214
  19.1 0.0 copy-done.1
  19.1 0.0 copy-done
  19.1 0.0 copy-start.3
  19.1 1.3 %image_spectrum.1.spec_ref = bf16[2,512,512]{2,1,0:T(8,128)(2,1)S(1)} custom-call(bf16[2,256,512]{2,1,0:T(8,128)(2,1)S(1)} %all_gather.8.top_ref, bf16[2,256,512]{2,1,0:T(8,128)(2,1)S(1)} %all_gather.9.low_ref, bf16[2,512,512]{2,1,0:T(8,128)(2,1)S(1)} %copy-done, bf16[2,512,512]{2,1,0:T(8,128)(2,1)S(1)} %copy-done.1), custom_call_target="tpu_custom_call" | custom-call | tf_op jit(solution)/shard_map/image_spectrum/pallas_call | solution.py:166
  20.4 0.0 copy-done.3
  20.5 1.7 %all-to-all-done.shares_ref = bf16[16,24,384]{2,1,0:T(8,128)(2,1)S(1)} async-done(((bf16[16,24,384]{2,1,0:T(8,128)(2,1)}), bf16[16,24,384]{2,1,0:T(8,128)(2,1)S(1)}, u32[]{:S(2)}, u32[]{:S(2)}) %all-to-all-start) | async-done | bytes 294944 | tf_op jit(solution)/shard_map/all_to_all | solution.py:202
  22.2 0.1 broadcast_in_dim.4.place_ref
  22.2 0.1 pick_place.1
  22.4 12.7 %all_to_all.20.shares_ref = bf16[4,2,24,384]{3,2,1,0:T(8,128)(2,1)S(1)} all-to-all(bf16[4,2,24,384]{3,2,1,0:T(8,128)(2,1)S(1)} %pick_place.1), channel_id=1, replica_groups={{4,6,0,2},{5,7,1,3},{12,14,8,10},{13,15,9,11},{20,22,16,18},{21,23,17,1..., dimensions={0} | all-to-all | bytes 294912 | tf_op jit(solution)/shard_map/all_to_all | solution.py:206
  35.1 0.1 broadcast_in_dim.5.place_ref
  35.2 15.9 %all_to_all.21.shares_ref = bf16[16,24,384]{2,1,0:T(8,128)(2,1)S(1)} all-to-all(bf16[16,24,384]{2,1,0:T(8,128)(2,1)S(1)} %pick_plane.1), channel_id=1, replica_groups={{32,33,56,57,16,17,40,41,0,1,24,25,48,49,8,9},{34,35,58,59,18,19,42,43,..., dimensions={0} | all-to-all | bytes 589824 | tf_op jit(solution)/shard_map/all_to_all | solution.py:209
  51.2 2.3 %correlate.1 = bf16[16,64,512]{2,1,0:T(8,128)(2,1)S(1)} custom-call(bf16[16,24,384]{2,1,0:T(8,128)(2,1)S(1)} %all_to_all.21.shares_ref, bf16[2,512,512]{2,1,0:T(8,128)(2,1)S(1)} %image_spectrum.1.spec_ref, bf16[2,512,512]{2,1,0:T(8,128)(2,1)S(1)} %copy-done, bf16[2,512,512]{2,1,0:T(8,128)(2,1)S(1)} %copy-done.1), custom_call_target="tpu_custom_call" | custom-call | tf_op jit(solution)/shard_map/correlate/pallas_call | solution.py:166
  53.5 18.9 %all_to_all.22.values_ref = bf16[16,64,512]{2,1,0:T(8,128)(2,1)S(1)} all-to-all(bf16[16,64,512]{2,1,0:T(8,128)(2,1)S(1)} %correlate.1), channel_id=1, replica_groups={{128,384,129,385,192,448,193,449,0,256,1,257,64,320,65,321},{130,386,13..., dimensions={0} | all-to-all | bytes 2097152 | tf_op jit(solution)/shard_map/all_to_all | solution.py:238
  72.4 1.0 %statistics.1 = (f32[1,64,512]{2,1,0:T(8,128)}, f32[1,64,512]{2,1,0:T(8,128)}, f32[1,64,512]{2,1,0:T(8,128)}) custom-call(bf16[16,64,512]{2,1,0:T(8,128)(2,1)S(1)} %all_to_all.22.values_ref), custom_call_target="tpu_custom_call" | custom-call | tf_op jit(solution)/shard_map/statistics/pallas_call | solution.py:166
  (3 shorter events, 0.1 us)
Async XLA Ops:
  0.6 13.9 %copy-start.2 = (bf16[1,512,512]{2,1,0:T(8,128)(2,1)S(1)}, bf16[1,512,512]{2,1,0:T(8,128)(2,1)}, u32[]{:S(2)}) copy-start(bf16[1,512,512]{2,1,0:T(8,128)(2,1)} %param.5) | copy-start | bytes 1572868
  0.6 21.5 %all-to-all-start = ((bf16[16,24,384]{2,1,0:T(8,128)(2,1)}), bf16[16,24,384]{2,1,0:T(8,128)(2,1)S(1)}, u32[]{:S(2)}, u32[]{:S(2)}) async-start(bf16[16,24,384]{2,1,0:T(8,128)(2,1)} %bitcast.25), calls=%async_computation | async-start | bytes 589824 | tf_op jit(solution)/shard_map/all_to_all | solution.py:202
  14.5 4.6 %copy-start.1 = (bf16[2,512,512]{2,1,0:T(8,128)(2,1)S(1)}, bf16[2,512,512]{2,1,0:T(8,128)(2,1)}, u32[]{:S(2)}) copy-start(bf16[2,512,512]{2,1,0:T(8,128)(2,1)} %constant.69.clone.inv_ref) | copy-start | bytes 3145732
  14.6 4.5 %copy-start = (bf16[2,512,512]{2,1,0:T(8,128)(2,1)S(1)}, bf16[2,512,512]{2,1,0:T(8,128)(2,1)}, u32[]{:S(2)}) copy-start(bf16[2,512,512]{2,1,0:T(8,128)(2,1)} %constant.68.clone.fwd_ref) | copy-start | bytes 3145732
  19.1 1.3 %copy-start.3 = (s32[1,2]{1,0:T(1,128)S(1)}, s32[1,2]{1,0:T(1,128)}, u32[]{:S(2)}) copy-start(s32[1,2]{1,0:T(1,128)} %param.7) | copy-start | bytes 28

commit v5 on v4

--- a/solution.py
+++ b/solution.py
@@ -187,7 +187,7 @@
 
 
 def result_members():
-    return [(zl * 4 + (x + 2) % 4, c) for x in range(4) for c in range(CORES) for zl in range(2)]
+    return [(zl * 4 + x, c) for x in (2, 3, 0, 1) for c in (1, 0) for zl in (1, 0)]
 
 
 def receive_template(own_template, owners, spec):

time: 73.8 us -> 73.6 us (level)
  no operation moved by 1% of the time
where the time goes in v5:
time: 73.6 us; the launch traced here: 73.2 us
  blocking collectives  51.8 us (70%)
  starting transfers between devices  13.9 us (19%)
  Pallas kernels  4.89 us (7%)
  waiting for transfers between devices  1.69 us (2%)
    all_to_all x1, blocking collectives, per_device(): lax.all_to_all(values, ('orient', 'tile'), 0, 0, axis_index_groups=across)  18.7 us
    all_to_all x1, blocking collectives, receive_template(): lax.all_to_all(shares, 'tile', 0, 0, axis_index_groups=gather_planes)  15.9 us
    all_to_all x1, starting transfers between devices, receive_template(): shares = lax.all_to_all(shares, 'tile', 0, 0, axis_index_groups=planes)  13.9 us
    all_to_all x1, blocking collectives, receive_template(): shares = lax.all_to_all(shares, 'tile', 0, 0, axis_index_groups=columns)  12.7 us
    pallas_call x5, Pallas kernels, call(): pl.pallas_call(kernel, name=name, out_shape=outs, in_specs=[whole] * len(...  4.89 us
    all_gather x2, blocking collectives, image_fields(): lax.all_gather(half, 'tile', axis_index_groups=pairs)  4.48 us
    all_to_all x1, waiting for transfers between devices, receive_template(): shares = lax.all_to_all(shares, 'tile', 0, 0, axis_index_groups=planes)  1.69 us
  transfers between devices with their start and end apart: 1, of which 1 were waited for; matrix products, arithmetic and copies ran while one was open for 0% of the time, Pallas kernels for 2%

profile of v5, /device:TPU:1, one launch (start us, length us, event | category | flops | bytes accessed | tf_op | source)
XLA Modules:
  0.0 73.2 jit_solution(1867967409495904270)
XLA Ops:
  0.6 0.0 copy-start.2
  0.6 13.9 %all-to-all-start = ((bf16[16,24,384]{2,1,0:T(8,128)(2,1)}), bf16[16,24,384]{2,1,0:T(8,128)(2,1)S(1)}, u32[]{:S(2)}, u32[]{:S(2)}) async-start(bf16[16,24,384]{2,1,0:T(8,128)(2,1)} %bitcast.25), calls=%async_computation | async-start | bytes 589824 | tf_op jit(solution)/shard_map/all_to_all | solution.py:202
  14.5 0.0 copy-done.2
  14.5 0.0 copy-start.1
  14.6 0.0 copy-start
  14.6 2.3 %all_gather.8.top_ref = bf16[2,256,512]{2,1,0:T(8,128)(2,1)S(1)} all-gather(bf16[1,256,512]{2,1,0:T(8,128)(2,1)S(1)} %get-tuple-element.8), channel_id=1, replica_groups={{0,1},{2,3},{4,5},{6,7},{8,9},{10,11},{12,13},{14,15},{16,17},{18,19},{..., dimensions={0}, use_global_device_ids=true | all-gather | bytes 786432 | tf_op jit(solution)/shard_map/all_gather | solution.py:214
  16.9 2.2 %all_gather.9.low_ref = bf16[2,256,512]{2,1,0:T(8,128)(2,1)S(1)} all-gather(bf16[1,256,512]{2,1,0:T(8,128)(2,1)S(1)} %get-tuple-element.7), channel_id=1, replica_groups={{0,1},{2,3},{4,5},{6,7},{8,9},{10,11},{12,13},{14,15},{16,17},{18,19},{..., dimensions={0}, use_global_device_ids=true | all-gather | bytes 786432 | tf_op jit(solution)/shard_map/all_gather | solution.py:214
  19.1 0.0 copy-done.1
  19.1 0.0 copy-done
  19.1 0.0 copy-start.3
  19.1 1.3 %image_spectrum.1.spec_ref = bf16[2,512,512]{2,1,0:T(8,128)(2,1)S(1)} custom-call(bf16[2,256,512]{2,1,0:T(8,128)(2,1)S(1)} %all_gather.8.top_ref, bf16[2,256,512]{2,1,0:T(8,128)(2,1)S(1)} %all_gather.9.low_ref, bf16[2,512,512]{2,1,0:T(8,128)(2,1)S(1)} %copy-done, bf16[2,512,512]{2,1,0:T(8,128)(2,1)S(1)} %copy-done.1), custom_call_target="tpu_custom_call" | custom-call | tf_op jit(solution)/shard_map/image_spectrum/pallas_call | solution.py:166
  20.4 0.0 copy-done.3
  20.5 1.7 %all-to-all-done.shares_ref = bf16[16,24,384]{2,1,0:T(8,128)(2,1)S(1)} async-done(((bf16[16,24,384]{2,1,0:T(8,128)(2,1)}), bf16[16,24,384]{2,1,0:T(8,128)(2,1)S(1)}, u32[]{:S(2)}, u32[]{:S(2)}) %all-to-all-start) | async-done | bytes 294944 | tf_op jit(solution)/shard_map/all_to_all | solution.py:202
  22.2 0.1 broadcast_in_dim.4.place_ref
  22.2 0.1 pick_place.1
  22.4 12.7 %all_to_all.20.shares_ref = bf16[4,2,24,384]{3,2,1,0:T(8,128)(2,1)S(1)} all-to-all(bf16[4,2,24,384]{3,2,1,0:T(8,128)(2,1)S(1)} %pick_place.1), channel_id=1, replica_groups={{4,6,0,2},{5,7,1,3},{12,14,8,10},{13,15,9,11},{20,22,16,18},{21,23,17,1..., dimensions={0} | all-to-all | bytes 294912 | tf_op jit(solution)/shard_map/all_to_all | solution.py:206
  35.1 0.1 broadcast_in_dim.5.place_ref
  35.2 15.9 %all_to_all.21.shares_ref = bf16[16,24,384]{2,1,0:T(8,128)(2,1)S(1)} all-to-all(bf16[16,24,384]{2,1,0:T(8,128)(2,1)S(1)} %pick_plane.1), channel_id=1, replica_groups={{32,33,56,57,16,17,40,41,0,1,24,25,48,49,8,9},{34,35,58,59,18,19,42,43,..., dimensions={0} | all-to-all | bytes 589824 | tf_op jit(solution)/shard_map/all_to_all | solution.py:209
  51.2 2.3 %correlate.1 = bf16[16,64,512]{2,1,0:T(8,128)(2,1)S(1)} custom-call(bf16[16,24,384]{2,1,0:T(8,128)(2,1)S(1)} %all_to_all.21.shares_ref, bf16[2,512,512]{2,1,0:T(8,128)(2,1)S(1)} %image_spectrum.1.spec_ref, bf16[2,512,512]{2,1,0:T(8,128)(2,1)S(1)} %copy-done, bf16[2,512,512]{2,1,0:T(8,128)(2,1)S(1)} %copy-done.1), custom_call_target="tpu_custom_call" | custom-call | tf_op jit(solution)/shard_map/correlate/pallas_call | solution.py:166
  53.5 18.7 %all_to_all.22.values_ref = bf16[16,64,512]{2,1,0:T(8,128)(2,1)S(1)} all-to-all(bf16[16,64,512]{2,1,0:T(8,128)(2,1)S(1)} %correlate.1), channel_id=1, replica_groups={{385,129,384,128,449,193,448,192,257,1,256,0,321,65,320,64},{387,131,38..., dimensions={0} | all-to-all | bytes 2097152 | tf_op jit(solution)/shard_map/all_to_all | solution.py:238
  72.2 1.0 %statistics.1 = (f32[1,64,512]{2,1,0:T(8,128)}, f32[1,64,512]{2,1,0:T(8,128)}, f32[1,64,512]{2,1,0:T(8,128)}) custom-call(bf16[16,64,512]{2,1,0:T(8,128)(2,1)S(1)} %all_to_all.22.values_ref), custom_call_target="tpu_custom_call" | custom-call | tf_op jit(solution)/shard_map/statistics/pallas_call | solution.py:166
  (3 shorter events, 0.1 us)
Async XLA Ops:
  0.6 13.9 %copy-start.2 = (bf16[1,512,512]{2,1,0:T(8,128)(2,1)S(1)}, bf16[1,512,512]{2,1,0:T(8,128)(2,1)}, u32[]{:S(2)}) copy-start(bf16[1,512,512]{2,1,0:T(8,128)(2,1)} %param.5) | copy-start | bytes 1572868
  0.6 21.5 %all-to-all-start = ((bf16[16,24,384]{2,1,0:T(8,128)(2,1)}), bf16[16,24,384]{2,1,0:T(8,128)(2,1)S(1)}, u32[]{:S(2)}, u32[]{:S(2)}) async-start(bf16[16,24,384]{2,1,0:T(8,128)(2,1)} %bitcast.25), calls=%async_computation | async-start | bytes 589824 | tf_op jit(solution)/shard_map/all_to_all | solution.py:202
  14.5 4.6 %copy-start.1 = (bf16[2,512,512]{2,1,0:T(8,128)(2,1)S(1)}, bf16[2,512,512]{2,1,0:T(8,128)(2,1)}, u32[]{:S(2)}) copy-start(bf16[2,512,512]{2,1,0:T(8,128)(2,1)} %constant.69.clone.inv_ref) | copy-start | bytes 3145732
  14.6 4.5 %copy-start = (bf16[2,512,512]{2,1,0:T(8,128)(2,1)S(1)}, bf16[2,512,512]{2,1,0:T(8,128)(2,1)}, u32[]{:S(2)}) copy-start(bf16[2,512,512]{2,1,0:T(8,128)(2,1)} %constant.68.clone.fwd_ref) | copy-start | bytes 3145732
  19.1 1.3 %copy-start.3 = (s32[1,2]{1,0:T(1,128)S(1)}, s32[1,2]{1,0:T(1,128)}, u32[]{:S(2)}) copy-start(s32[1,2]{1,0:T(1,128)} %param.7) | copy-start | bytes 28

commit v6 on v5

--- a/solution.py
+++ b/solution.py
@@ -66,7 +66,7 @@
     for step in range(STEPS):
         share = pick(shares_ref, place_ref, step)
         for y in range(Y):
-            out_ref[gather_members().index((y, step))] = share
+            out_ref[plane_place(y, step)] = share
 
 
 def side_by_side(left, col_parity):
@@ -96,9 +96,8 @@
 
 
 def correlate_kernel(shares_ref, spec_ref, fwd_ref, inv_ref, out_ref, field_ref, back_ref):
-    for source, member in enumerate(gather_members()):
-        place = plane_place(*member)
-        field_ref[place * CHUNK : (place + 1) * CHUNK, :] = wide(shares_ref[source])
+    for place in range(PLANE):
+        field_ref[place * CHUNK : (place + 1) * CHUNK, :] = wide(shares_ref[place])
     left = []
     for row_parity in (0, 1):
         top = combine(field_ref[:REST], field_ref[HALF:], row_parity)
@@ -175,38 +174,40 @@
 
 
 def plane_place(y, core):
-    return (3 * y + 4) % Y * CORES + core
-
-
-def gather_members():
+    return (3 * y + 4) % Y * CORES + 1 - core
+
+
+def column_place(z):
+    return 2 * (z % 2) + 1 - z // 2
+
+
+def plane_members():
     return sorted(((y, c) for y in range(Y) for c in range(CORES)), key=lambda member: plane_place(*member))
 
 
-def column_place(z):
-    return (z + 2) % Z
+def column_members():
+    return sorted(range(Z), key=column_place)
 
 
 def result_members():
-    return [(zl * 4 + x, c) for x in (2, 3, 0, 1) for c in (1, 0) for zl in (1, 0)]
+    return [(z_lo * 4 + x, c) for x in (2, 3, 0, 1) for c in (1, 0) for z_lo in (1, 0)]
 
 
 def receive_template(own_template, owners, spec):
-    plane_members = sorted(((y, c) for y in range(Y) for c in range(CORES)), key=lambda member: plane_place(*member))
-    planes = [[(y * Z + z) * CORES + c for y, c in plane_members] for z in range(Z)]
-    gather_planes = [[(y * Z + z) * CORES + c for y, c in gather_members()] for z in range(Z)]
-    columns = [[(y * Z + z) * CORES + c for z in sorted(range(Z), key=column_place)] for y in range(Y) for c in range(CORES)]
+    planes = [[(y * Z + z) * CORES + c for y, c in plane_members()] for z in range(Z)]
+    columns = [[(y * Z + z) * CORES + c for z in column_members()] for y in range(Y) for c in range(CORES)]
     owner_z = column_place(owners // CORES % Z)
     owner_place = plane_place(owners // (Z * CORES), owners % CORES)
     owner_z, owner_place = (jnp.broadcast_to(place[:, None], (STEPS, M)) for place in (owner_z, owner_place))
     shares = own_template.reshape(PLANE, CHUNK, M)
     shares = lax.all_to_all(shares, "tile", 0, 0, axis_index_groups=planes)
-    shares, spec = lax.optimization_barrier((shares, spec))
+    shares, spec, owner_z, owner_place = lax.optimization_barrier((shares, spec, owner_z, owner_place))
     spread = jax.ShapeDtypeStruct((Z, STEPS, CHUNK, M), jnp.bfloat16)
     shares = call(pick_place_kernel, "pick_place", spread, [], shares, owner_place)
     shares = lax.all_to_all(shares, "tile", 0, 0, axis_index_groups=columns)
     spread = jax.ShapeDtypeStruct((PLANE, CHUNK, M), jnp.bfloat16)
     shares = call(pick_plane_kernel, "pick_plane", spread, [], shares, owner_z)
-    return lax.all_to_all(shares, "tile", 0, 0, axis_index_groups=gather_planes), spec
+    return lax.all_to_all(shares, "tile", 0, 0, axis_index_groups=planes), spec
 
 
 def image_fields(own_tile):

time: 73.6 us -> 72.4 us (0.984)
  no operation moved by 1% of the time
where the time goes in v6:
time: 72.4 us; the launch traced here: 72 us
  blocking collectives  51.1 us (71%)
  starting transfers between devices  13.6 us (19%)
  Pallas kernels  4.89 us (7%)
  waiting for transfers between devices  1.57 us (2%)
    all_to_all x1, blocking collectives, per_device(): lax.all_to_all(values, ('orient', 'tile'), 0, 0, axis_index_groups=across)  18.7 us
    all_to_all x1, blocking collectives, receive_template(): lax.all_to_all(shares, 'tile', 0, 0, axis_index_groups=planes)  15.8 us
    all_to_all x1, starting transfers between devices, receive_template(): shares = lax.all_to_all(shares, 'tile', 0, 0, axis_index_groups=planes)  13.6 us
    all_to_all x1, blocking collectives, receive_template(): shares = lax.all_to_all(shares, 'tile', 0, 0, axis_index_groups=columns)  12 us
    pallas_call x5, Pallas kernels, call(): pl.pallas_call(kernel, name=name, out_shape=outs, in_specs=[whole] * len(...  4.89 us
    all_gather x2, blocking collectives, image_fields(): lax.all_gather(half, 'tile', axis_index_groups=pairs)  4.54 us
    all_to_all x1, waiting for transfers between devices, receive_template(): shares = lax.all_to_all(shares, 'tile', 0, 0, axis_index_groups=planes)  1.57 us
  transfers between devices with their start and end apart: 1, of which 1 were waited for; matrix products, arithmetic and copies ran while one was open for 0% of the time, Pallas kernels for 2%

profile of v6, /device:TPU:1, one launch (start us, length us, event | category | flops | bytes accessed | tf_op | source)
XLA Modules:
  0.0 72.0 jit_solution(16446888819182052947)
XLA Ops:
  0.6 0.0 copy-start.2
  0.6 13.6 %all-to-all-start = ((bf16[16,24,384]{2,1,0:T(8,128)(2,1)}), bf16[16,24,384]{2,1,0:T(8,128)(2,1)S(1)}, u32[]{:S(2)}, u32[]{:S(2)}) async-start(bf16[16,24,384]{2,1,0:T(8,128)(2,1)} %bitcast.25), calls=%async_computation | async-start | bytes 589824 | tf_op jit(solution)/shard_map/all_to_all | solution.py:203
  14.2 0.0 copy-done.2
  14.2 0.0 copy-start.1
  14.3 0.0 copy-start
  14.3 2.4 %all_gather.8.top_ref = bf16[2,256,512]{2,1,0:T(8,128)(2,1)S(1)} all-gather(bf16[1,256,512]{2,1,0:T(8,128)(2,1)S(1)} %get-tuple-element.12), channel_id=1, replica_groups={{0,1},{2,3},{4,5},{6,7},{8,9},{10,11},{12,13},{14,15},{16,17},{18,19},{..., dimensions={0}, use_global_device_ids=true | all-gather | bytes 786432 | tf_op jit(solution)/shard_map/all_gather | solution.py:215
  16.7 2.2 %all_gather.9.low_ref = bf16[2,256,512]{2,1,0:T(8,128)(2,1)S(1)} all-gather(bf16[1,256,512]{2,1,0:T(8,128)(2,1)S(1)} %get-tuple-element.11), channel_id=1, replica_groups={{0,1},{2,3},{4,5},{6,7},{8,9},{10,11},{12,13},{14,15},{16,17},{18,19},{..., dimensions={0}, use_global_device_ids=true | all-gather | bytes 786432 | tf_op jit(solution)/shard_map/all_gather | solution.py:215
  18.8 0.0 copy-done.1
  18.8 0.0 copy-done
  18.8 0.0 copy-start.3
  18.8 1.3 %image_spectrum.1.spec_ref = bf16[2,512,512]{2,1,0:T(8,128)(2,1)S(1)} custom-call(bf16[2,256,512]{2,1,0:T(8,128)(2,1)S(1)} %all_gather.8.top_ref, bf16[2,256,512]{2,1,0:T(8,128)(2,1)S(1)} %all_gather.9.low_ref, bf16[2,512,512]{2,1,0:T(8,128)(2,1)S(1)} %copy-done, bf16[2,512,512]{2,1,0:T(8,128)(2,1)S(1)} %copy-done.1), custom_call_target="tpu_custom_call" | custom-call | tf_op jit(solution)/shard_map/image_spectrum/pallas_call | solution.py:165
  20.2 0.0 copy-done.3
  20.2 1.6 %all-to-all-done.shares_ref = bf16[16,24,384]{2,1,0:T(8,128)(2,1)S(1)} async-done(((bf16[16,24,384]{2,1,0:T(8,128)(2,1)}), bf16[16,24,384]{2,1,0:T(8,128)(2,1)S(1)}, u32[]{:S(2)}, u32[]{:S(2)}) %all-to-all-start) | async-done | bytes 294944 | tf_op jit(solution)/shard_map/all_to_all | solution.py:203
  21.8 0.1 broadcast_in_dim.4.place_ref
  21.9 0.1 broadcast_in_dim.5.place_ref
  21.9 0.1 pick_place.1
  22.1 12.0 %all_to_all.20.shares_ref = bf16[4,2,24,384]{3,2,1,0:T(8,128)(2,1)S(1)} all-to-all(bf16[4,2,24,384]{3,2,1,0:T(8,128)(2,1)S(1)} %pick_place.1), channel_id=1, replica_groups={{4,0,6,2},{5,1,7,3},{12,8,14,10},{13,9,15,11},{20,16,22,18},{21,17,23,1..., dimensions={0} | all-to-all | bytes 294912 | tf_op jit(solution)/shard_map/all_to_all | solution.py:207
  34.1 15.8 %all_to_all.21.shares_ref = bf16[16,24,384]{2,1,0:T(8,128)(2,1)S(1)} all-to-all(bf16[16,24,384]{2,1,0:T(8,128)(2,1)S(1)} %pick_plane.1), channel_id=1, replica_groups={{33,32,57,56,17,16,41,40,1,0,25,24,49,48,9,8},{35,34,59,58,19,18,43,42,..., dimensions={0} | all-to-all | bytes 589824 | tf_op jit(solution)/shard_map/all_to_all | solution.py:210
  50.0 2.3 %correlate.1 = bf16[16,64,512]{2,1,0:T(8,128)(2,1)S(1)} custom-call(bf16[16,24,384]{2,1,0:T(8,128)(2,1)S(1)} %all_to_all.21.shares_ref, bf16[2,512,512]{2,1,0:T(8,128)(2,1)S(1)} %image_spectrum.1.spec_ref, bf16[2,512,512]{2,1,0:T(8,128)(2,1)S(1)} %copy-done, bf16[2,512,512]{2,1,0:T(8,128)(2,1)S(1)} %copy-done.1), custom_call_target="tpu_custom_call" | custom-call | tf_op jit(solution)/shard_map/correlate/pallas_call | solution.py:165
  52.3 18.7 %all_to_all.22.values_ref = bf16[16,64,512]{2,1,0:T(8,128)(2,1)S(1)} all-to-all(bf16[16,64,512]{2,1,0:T(8,128)(2,1)S(1)} %correlate.1), channel_id=1, replica_groups={{385,129,384,128,449,193,448,192,257,1,256,0,321,65,320,64},{387,131,38..., dimensions={0} | all-to-all | bytes 2097152 | tf_op jit(solution)/shard_map/all_to_all | solution.py:239
  71.0 1.0 %statistics.1 = (f32[1,64,512]{2,1,0:T(8,128)}, f32[1,64,512]{2,1,0:T(8,128)}, f32[1,64,512]{2,1,0:T(8,128)}) custom-call(bf16[16,64,512]{2,1,0:T(8,128)(2,1)S(1)} %all_to_all.22.values_ref), custom_call_target="tpu_custom_call" | custom-call | tf_op jit(solution)/shard_map/statistics/pallas_call | solution.py:165
  (3 shorter events, 0.1 us)
Async XLA Ops:
  0.6 13.6 %copy-start.2 = (bf16[1,512,512]{2,1,0:T(8,128)(2,1)S(1)}, bf16[1,512,512]{2,1,0:T(8,128)(2,1)}, u32[]{:S(2)}) copy-start(bf16[1,512,512]{2,1,0:T(8,128)(2,1)} %param.5) | copy-start | bytes 1572868
  0.6 21.1 %all-to-all-start = ((bf16[16,24,384]{2,1,0:T(8,128)(2,1)}), bf16[16,24,384]{2,1,0:T(8,128)(2,1)S(1)}, u32[]{:S(2)}, u32[]{:S(2)}) async-start(bf16[16,24,384]{2,1,0:T(8,128)(2,1)} %bitcast.25), calls=%async_computation | async-start | bytes 589824 | tf_op jit(solution)/shard_map/all_to_all | solution.py:203
  14.2 4.6 %copy-start.1 = (bf16[2,512,512]{2,1,0:T(8,128)(2,1)S(1)}, bf16[2,512,512]{2,1,0:T(8,128)(2,1)}, u32[]{:S(2)}) copy-start(bf16[2,512,512]{2,1,0:T(8,128)(2,1)} %constant.77.clone.inv_ref) | copy-start | bytes 3145732
  14.3 4.6 %copy-start = (bf16[2,512,512]{2,1,0:T(8,128)(2,1)S(1)}, bf16[2,512,512]{2,1,0:T(8,128)(2,1)}, u32[]{:S(2)}) copy-start(bf16[2,512,512]{2,1,0:T(8,128)(2,1)} %constant.76.clone.fwd_ref) | copy-start | bytes 3145732
  18.8 1.3 %copy-start.3 = (s32[1,2]{1,0:T(1,128)S(1)}, s32[1,2]{1,0:T(1,128)}, u32[]{:S(2)}) copy-start(s32[1,2]{1,0:T(1,128)} %param.7) | copy-start | bytes 28

commit v7 on v6

--- a/solution.py
+++ b/solution.py
@@ -74,12 +74,17 @@
     return jnp.concatenate([jnp.concatenate([a[:HALF, cols], a[HALF:, cols]], axis=1) for a in left], axis=0)
 
 
-def image_kernel(top_ref, low_ref, fwd_ref, inv_ref, spec_ref):
+def image_kernel(top_ref, low_ref, fwd_ref, inv_ref, spec_ref, level_ref):
     quarters = []
     for core in range(CORES):
-        top_left, top_right = wide(top_ref[core, :, :HALF]), wide(top_ref[core, :, HALF:])
-        low_left, low_right = wide(low_ref[core, :, :HALF]), wide(low_ref[core, :, HALF:])
-        quarters.append((top_left, top_right, low_left, low_right))
+        top, low = wide(top_ref[core]), wide(low_ref[core])
+        energy = jnp.sum(top * top + low * low, axis=0, keepdims=True)
+        energy = jnp.sum(energy, axis=1, keepdims=True)
+        level = jnp.where(energy > 0, jnp.sqrt(energy * jnp.float32(1.0 / (NP * NP))), 1.0)
+        level = jnp.where(level > 0, level, 1.0)
+        level_ref[core : core + 1, :] = jnp.broadcast_to(level, (1, NP))
+        top, low = top / level, low / level
+        quarters.append((top[:, :HALF], top[:, HALF:], low[:, :HALF], low[:, HALF:]))
     left = []
     for row_parity in (0, 1):
         folded = []
@@ -148,16 +153,16 @@
     return values[0]
 
 
-def statistics_kernel(values_ref, total_ref, squares_ref, largest_ref):
-    scale = 1.0 / (NP * NP)
+def statistics_kernel(values_ref, level_ref, total_ref, squares_ref, largest_ref):
+    scale = level_ref[...] * jnp.float32(1.0 / (NP * NP))
     count, height, width = values_ref.shape
     for row in range(0, height, 16):
         for col in range(0, width, 128):
             rows, cols = slice(row, row + 16), slice(col, col + 128)
             values = [wide(values_ref[template, rows, cols]) for template in range(count)]
-            total_ref[0, rows, cols] = pairwise(jnp.add, values) * jnp.float32(scale)
-            squares_ref[0, rows, cols] = pairwise(jnp.add, [v * v for v in values]) * jnp.float32(scale * scale)
-            largest_ref[0, rows, cols] = pairwise(jnp.maximum, values) * jnp.float32(scale)
+            total_ref[0, rows, cols] = pairwise(jnp.add, values) * scale[:, cols]
+            squares_ref[0, rows, cols] = pairwise(jnp.add, [v * v for v in values]) * (scale * scale)[:, cols]
+            largest_ref[0, rows, cols] = pairwise(jnp.maximum, values) * scale[:, cols]
 
 
 def call(kernel, name, outs, scratch, *operands):
@@ -193,7 +198,7 @@
     return [(z_lo * 4 + x, c) for x in (2, 3, 0, 1) for c in (1, 0) for z_lo in (1, 0)]
 
 
-def receive_template(own_template, owners, spec):
+def receive_template(own_template, owners, spec, own_level):
     planes = [[(y * Z + z) * CORES + c for y, c in plane_members()] for z in range(Z)]
     columns = [[(y * Z + z) * CORES + c for z in column_members()] for y in range(Y) for c in range(CORES)]
     owner_z = column_place(owners // CORES % Z)
@@ -201,13 +206,15 @@
     owner_z, owner_place = (jnp.broadcast_to(place[:, None], (STEPS, M)) for place in (owner_z, owner_place))
     shares = own_template.reshape(PLANE, CHUNK, M)
     shares = lax.all_to_all(shares, "tile", 0, 0, axis_index_groups=planes)
-    shares, spec, owner_z, owner_place = lax.optimization_barrier((shares, spec, owner_z, owner_place))
+    shares, spec, own_level, owner_z, owner_place = lax.optimization_barrier(
+        (shares, spec, own_level, owner_z, owner_place)
+    )
     spread = jax.ShapeDtypeStruct((Z, STEPS, CHUNK, M), jnp.bfloat16)
     shares = call(pick_place_kernel, "pick_place", spread, [], shares, owner_place)
     shares = lax.all_to_all(shares, "tile", 0, 0, axis_index_groups=columns)
     spread = jax.ShapeDtypeStruct((PLANE, CHUNK, M), jnp.bfloat16)
     shares = call(pick_plane_kernel, "pick_plane", spread, [], shares, owner_z)
-    return lax.all_to_all(shares, "tile", 0, 0, axis_index_groups=planes), spec
+    return lax.all_to_all(shares, "tile", 0, 0, axis_index_groups=planes), spec, own_level
 
 
 def image_fields(own_tile):
@@ -223,8 +230,10 @@
     rows_out = NP // groups_here
     spectrum = (2, NP, NP)
     fields = image_fields(image_tiles[0])
-    spec = call(image_kernel, "image_spectrum", jax.ShapeDtypeStruct(spectrum, jnp.bfloat16), [], *fields, fwd, inv)
-    shares, spec = receive_template(templates[0, 0], owners[0], spec)
+    image_outs = (jax.ShapeDtypeStruct(spectrum, jnp.bfloat16), jax.ShapeDtypeStruct((CORES, NP), jnp.float32))
+    spec, levels = call(image_kernel, "image_spectrum", image_outs, [], *fields, fwd, inv)
+    own_level = jnp.where(lax.axis_index("tile") % CORES == 0, levels[:1], levels[1:])
+    shares, spec, own_level = receive_template(templates[0, 0], owners[0], spec, own_level)
     values = call(
         correlate_kernel,
         "correlate",
@@ -238,7 +247,7 @@
     across = [[group * tiles + pair * CORES + c for group, c in result_members()] for pair in range(tiles // CORES)]
     values = lax.all_to_all(values, ("orient", "tile"), 0, 0, axis_index_groups=across)
     out = jax.ShapeDtypeStruct((1, rows_out, NP), jnp.float32)
-    return call(statistics_kernel, "statistics", (out, out, out), [], values)
+    return call(statistics_kernel, "statistics", (out, out, out), [], values, own_level)
 
 
 def solution(mesh):

time: 72.4 us -> 72.4 us (level)
  no operation moved by 1% of the time
where the time goes in v7:
time: 72.4 us; the launch traced here: 72 us
  blocking collectives  51.1 us (71%)
  starting transfers between devices  13.6 us (19%)
  Pallas kernels  5.22 us (7%)
  waiting for transfers between devices  1.23 us (2%)
    all_to_all x1, blocking collectives, per_device(): lax.all_to_all(values, ('orient', 'tile'), 0, 0, axis_index_groups=across)  18.7 us
    all_to_all x1, blocking collectives, receive_template(): lax.all_to_all(shares, 'tile', 0, 0, axis_index_groups=planes)  15.8 us
    all_to_all x1, starting transfers between devices, receive_template(): shares = lax.all_to_all(shares, 'tile', 0, 0, axis_index_groups=planes)  13.6 us
    all_to_all x1, blocking collectives, receive_template(): shares = lax.all_to_all(shares, 'tile', 0, 0, axis_index_groups=columns)  12 us
    pallas_call x5, Pallas kernels, call(): pl.pallas_call(kernel, name=name, out_shape=outs, in_specs=[whole] * len(...  5.22 us
    all_gather x2, blocking collectives, image_fields(): lax.all_gather(half, 'tile', axis_index_groups=pairs)  4.54 us
  transfers between devices with their start and end apart: 1, of which 1 were waited for; matrix products, arithmetic and copies ran while one was open for 0% of the time, Pallas kernels for 2%

profile of v7, /device:TPU:1, one launch (start us, length us, event | category | flops | bytes accessed | tf_op | source)
XLA Modules:
  0.0 72.0 jit_solution(7143796411681704956)
XLA Ops:
  0.6 0.0 copy-start.2
  0.6 13.6 %all-to-all-start = ((bf16[16,24,384]{2,1,0:T(8,128)(2,1)}), bf16[16,24,384]{2,1,0:T(8,128)(2,1)S(1)}, u32[]{:S(2)}, u32[]{:S(2)}) async-start(bf16[16,24,384]{2,1,0:T(8,128)(2,1)} %bitcast.25), calls=%async_computation | async-start | bytes 589824 | tf_op jit(solution)/shard_map/all_to_all | solution.py:208
  14.2 0.0 copy-done.2
  14.2 0.0 copy-start.1
  14.3 0.0 copy-start
  14.3 2.4 %all_gather.8.top_ref = bf16[2,256,512]{2,1,0:T(8,128)(2,1)S(1)} all-gather(bf16[1,256,512]{2,1,0:T(8,128)(2,1)S(1)} %get-tuple-element.18), channel_id=1, replica_groups={{0,1},{2,3},{4,5},{6,7},{8,9},{10,11},{12,13},{14,15},{16,17},{18,19},{..., dimensions={0}, use_global_device_ids=true | all-gather | bytes 786432 | tf_op jit(solution)/shard_map/all_gather | solution.py:222
  16.7 2.2 %all_gather.9.low_ref = bf16[2,256,512]{2,1,0:T(8,128)(2,1)S(1)} all-gather(bf16[1,256,512]{2,1,0:T(8,128)(2,1)S(1)} %get-tuple-element.17), channel_id=1, replica_groups={{0,1},{2,3},{4,5},{6,7},{8,9},{10,11},{12,13},{14,15},{16,17},{18,19},{..., dimensions={0}, use_global_device_ids=true | all-gather | bytes 786432 | tf_op jit(solution)/shard_map/all_gather | solution.py:222
  18.8 0.0 copy-done.1
  18.8 0.0 copy-done
  18.8 0.0 copy-start.3
  18.8 1.7 %image_spectrum.1 = (bf16[2,512,512]{2,1,0:T(8,128)(2,1)S(1)}, f32[2,512]{1,0:T(2,128)S(1)}) custom-call(bf16[2,256,512]{2,1,0:T(8,128)(2,1)S(1)} %all_gather.8.top_ref, bf16[2,256,512]{2,1,0:T(8,128)(2,1)S(1)} %all_gather.9.low_ref, bf16[2,512,512]{2,1,0:T(8,128)(2,1)S(1)} %copy-done, bf16[2,512,512]{2,1,0:T(8,128)(2,1)S(1)} %copy-done.1), custom_call_target="tpu_custom_call" | custom-call | tf_op jit(solution)/shard_map/image_spectrum/pallas_call | solution.py:170
  20.5 0.0 copy-done.3
  20.6 1.2 %all-to-all-done.shares_ref = bf16[16,24,384]{2,1,0:T(8,128)(2,1)S(1)} async-done(((bf16[16,24,384]{2,1,0:T(8,128)(2,1)}), bf16[16,24,384]{2,1,0:T(8,128)(2,1)S(1)}, u32[]{:S(2)}, u32[]{:S(2)}) %all-to-all-start) | async-done | bytes 294944 | tf_op jit(solution)/shard_map/all_to_all | solution.py:208
  21.8 0.1 broadcast_in_dim.4.place_ref
  21.9 0.1 broadcast_in_dim.5.place_ref
  21.9 0.1 pick_place.1
  22.1 12.0 %all_to_all.20.shares_ref = bf16[4,2,24,384]{3,2,1,0:T(8,128)(2,1)S(1)} all-to-all(bf16[4,2,24,384]{3,2,1,0:T(8,128)(2,1)S(1)} %pick_place.1), channel_id=1, replica_groups={{4,0,6,2},{5,1,7,3},{12,8,14,10},{13,9,15,11},{20,16,22,18},{21,17,23,1..., dimensions={0} | all-to-all | bytes 294912 | tf_op jit(solution)/shard_map/all_to_all | solution.py:214
  34.1 15.8 %all_to_all.21.shares_ref = bf16[16,24,384]{2,1,0:T(8,128)(2,1)S(1)} all-to-all(bf16[16,24,384]{2,1,0:T(8,128)(2,1)S(1)} %pick_plane.1), channel_id=1, replica_groups={{33,32,57,56,17,16,41,40,1,0,25,24,49,48,9,8},{35,34,59,58,19,18,43,42,..., dimensions={0} | all-to-all | bytes 589824 | tf_op jit(solution)/shard_map/all_to_all | solution.py:217
  50.0 2.3 %correlate.1 = bf16[16,64,512]{2,1,0:T(8,128)(2,1)S(1)} custom-call(bf16[16,24,384]{2,1,0:T(8,128)(2,1)S(1)} %all_to_all.21.shares_ref, bf16[2,512,512]{2,1,0:T(8,128)(2,1)S(1)} %get-tuple-element.15.spec_ref, bf16[2,512,512]{2,1,0:T(8,128)(2,1)S(1)} %copy-done, bf16[2,512,512]{2,1,0:T(8,128)(2,1)S(1)} %copy-done.1), custom_call_target="tpu_custom_call" | custom-call | tf_op jit(solution)/shard_map/correlate/pallas_call | solution.py:170
  52.3 18.7 %all_to_all.22.values_ref = bf16[16,64,512]{2,1,0:T(8,128)(2,1)S(1)} all-to-all(bf16[16,64,512]{2,1,0:T(8,128)(2,1)S(1)} %correlate.1), channel_id=1, replica_groups={{385,129,384,128,449,193,448,192,257,1,256,0,321,65,320,64},{387,131,38..., dimensions={0} | all-to-all | bytes 2097152 | tf_op jit(solution)/shard_map/all_to_all | solution.py:248
  71.0 1.0 %statistics.1 = (f32[1,64,512]{2,1,0:T(8,128)}, f32[1,64,512]{2,1,0:T(8,128)}, f32[1,64,512]{2,1,0:T(8,128)}) custom-call(bf16[16,64,512]{2,1,0:T(8,128)(2,1)S(1)} %all_to_all.22.values_ref, f32[1,512]{1,0:T(1,128)S(1)} %broadcast_select_fusion.level_ref), custom_call_target="tpu_custom_call" | custom-call | tf_op jit(solution)/shard_map/statistics/pallas_call | solution.py:170
  (4 shorter events, 0.1 us)
Async XLA Ops:
  0.6 13.6 %copy-start.2 = (bf16[1,512,512]{2,1,0:T(8,128)(2,1)S(1)}, bf16[1,512,512]{2,1,0:T(8,128)(2,1)}, u32[]{:S(2)}) copy-start(bf16[1,512,512]{2,1,0:T(8,128)(2,1)} %param.5) | copy-start | bytes 1572868
  0.6 21.1 %all-to-all-start = ((bf16[16,24,384]{2,1,0:T(8,128)(2,1)}), bf16[16,24,384]{2,1,0:T(8,128)(2,1)S(1)}, u32[]{:S(2)}, u32[]{:S(2)}) async-start(bf16[16,24,384]{2,1,0:T(8,128)(2,1)} %bitcast.25), calls=%async_computation | async-start | bytes 589824 | tf_op jit(solution)/shard_map/all_to_all | solution.py:208
  14.2 4.6 %copy-start.1 = (bf16[2,512,512]{2,1,0:T(8,128)(2,1)S(1)}, bf16[2,512,512]{2,1,0:T(8,128)(2,1)}, u32[]{:S(2)}) copy-start(bf16[2,512,512]{2,1,0:T(8,128)(2,1)} %constant.88.clone.inv_ref) | copy-start | bytes 3145732
  14.3 4.6 %copy-start = (bf16[2,512,512]{2,1,0:T(8,128)(2,1)S(1)}, bf16[2,512,512]{2,1,0:T(8,128)(2,1)}, u32[]{:S(2)}) copy-start(bf16[2,512,512]{2,1,0:T(8,128)(2,1)} %constant.87.clone.fwd_ref) | copy-start | bytes 3145732
  18.8 1.7 %copy-start.3 = (s32[1,2]{1,0:T(1,128)S(1)}, s32[1,2]{1,0:T(1,128)}, u32[]{:S(2)}) copy-start(s32[1,2]{1,0:T(1,128)} %param.7) | copy-start | bytes 28

commit v8 on v7

--- a/solution.py
+++ b/solution.py
@@ -100,13 +100,12 @@
         spec_ref[col_parity] = narrow(matmul(side_by_side(left, col_parity), inv_ref[col_parity]))
 
 
-def correlate_kernel(shares_ref, spec_ref, fwd_ref, inv_ref, out_ref, field_ref, back_ref):
-    for place in range(PLANE):
-        field_ref[place * CHUNK : (place + 1) * CHUNK, :] = wide(shares_ref[place])
+def correlate_kernel(shares_ref, spec_ref, fwd_ref, inv_ref, out_ref, back_ref):
+    field = jnp.concatenate([wide(shares_ref[place]) for place in range(PLANE)], axis=0)
     left = []
     for row_parity in (0, 1):
-        top = combine(field_ref[:REST], field_ref[HALF:], row_parity)
-        rows = jnp.concatenate([top, field_ref[REST:HALF]], axis=0)
+        top = combine(field[:REST], field[HALF:], row_parity)
+        rows = jnp.concatenate([top, field[REST:HALF]], axis=0)
         folded = []
         for col_parity in (0, 1):
             first = combine(rows[:, :REST], rows[:, HALF:], col_parity)
@@ -203,7 +202,7 @@
     columns = [[(y * Z + z) * CORES + c for z in column_members()] for y in range(Y) for c in range(CORES)]
     owner_z = column_place(owners // CORES % Z)
     owner_place = plane_place(owners // (Z * CORES), owners % CORES)
-    owner_z, owner_place = (jnp.broadcast_to(place[:, None], (STEPS, M)) for place in (owner_z, owner_place))
+    owner_z, owner_place = owner_z[:, None], owner_place[:, None]
     shares = own_template.reshape(PLANE, CHUNK, M)
     shares = lax.all_to_all(shares, "tile", 0, 0, axis_index_groups=planes)
     shares, spec, own_level, owner_z, owner_place = lax.optimization_barrier(
@@ -238,7 +237,7 @@
         correlate_kernel,
         "correlate",
         jax.ShapeDtypeStruct((groups_here * CORES, rows_out, NP), jnp.bfloat16),
-        [pltpu.VMEM((M, M), jnp.float32), pltpu.VMEM(spectrum, jnp.float32)],
+        [pltpu.VMEM(spectrum, jnp.float32)],
         shares,
         spec,
         fwd,

time: 72.4 us -> 72.4 us (level)
  waiting for transfers between devices: 1.23 us -> 0.16 us
  local copies, waits for them, and re-layouts: 0.2 us -> 1.12 us
    all_to_all x1, waiting for transfers between devices: 1.23 us -> 0.16 us  [receive_template(): shares = lax.all_to_all(shares, 'tile', 0, 0, axis_index_groups=planes)]
    unnamed x8 -> x12, local copies, waits for them, and re-layouts: 0.02 us -> 1 us
where the time goes in v8:
time: 72.4 us; the launch traced here: 72.1 us
  blocking collectives  51.2 us (71%)
  starting transfers between devices  13.6 us (19%)
  Pallas kernels  5.26 us (7%)
  local copies, waits for them, and re-layouts  1.12 us (2%)
  between operations  0.73 us (1%)
    all_to_all x1, blocking collectives, per_device(): lax.all_to_all(values, ('orient', 'tile'), 0, 0, axis_index_groups=across)  18.7 us
    all_to_all x1, blocking collectives, receive_template(): lax.all_to_all(shares, 'tile', 0, 0, axis_index_groups=planes)  15.8 us
    all_to_all x1, starting transfers between devices, receive_template(): shares = lax.all_to_all(shares, 'tile', 0, 0, axis_index_groups=planes)  13.6 us
    all_to_all x1, blocking collectives, receive_template(): shares = lax.all_to_all(shares, 'tile', 0, 0, axis_index_groups=columns)  12.1 us
    pallas_call x5, Pallas kernels, call(): pl.pallas_call(kernel, name=name, out_shape=outs, in_specs=[whole] * len(...  5.26 us
    all_gather x2, blocking collectives, image_fields(): lax.all_gather(half, 'tile', axis_index_groups=pairs)  4.54 us
  transfers between devices with their start and end apart: 1, of which 1 were waited for; matrix products, arithmetic and copies ran while one was open for 0% of the time, Pallas kernels for 2%

profile of v8, /device:TPU:1, one launch (start us, length us, event | category | flops | bytes accessed | tf_op | source)
XLA Modules:
  0.0 72.1 jit_solution(18053798326783729429)
XLA Ops:
  0.6 0.0 copy-start.4
  0.6 13.6 %all-to-all-start = ((bf16[16,24,384]{2,1,0:T(8,128)(2,1)}), bf16[16,24,384]{2,1,0:T(8,128)(2,1)S(1)}, u32[]{:S(2)}, u32[]{:S(2)}) async-start(bf16[16,24,384]{2,1,0:T(8,128)(2,1)} %bitcast.2), calls=%async_computation | async-start | bytes 589824 | tf_op jit(solution)/shard_map/all_to_all | solution.py:207
  14.2 0.0 copy-done.4
  14.2 0.0 copy-start.5
  14.2 0.0 copy-start.1
  14.3 0.0 copy-start
  14.3 2.4 %all_gather.8.top_ref = bf16[2,256,512]{2,1,0:T(8,128)(2,1)S(1)} all-gather(bf16[1,256,512]{2,1,0:T(8,128)(2,1)S(1)} %get-tuple-element.18), channel_id=1, replica_groups={{0,1},{2,3},{4,5},{6,7},{8,9},{10,11},{12,13},{14,15},{16,17},{18,19},{..., dimensions={0}, use_global_device_ids=true | all-gather | bytes 786432 | tf_op jit(solution)/shard_map/all_gather | solution.py:221
  16.7 0.0 copy-done.5
  16.7 0.1 copy.12
  16.8 2.2 %all_gather.9.low_ref = bf16[2,256,512]{2,1,0:T(8,128)(2,1)S(1)} all-gather(bf16[1,256,512]{2,1,0:T(8,128)(2,1)S(1)} %get-tuple-element.17), channel_id=1, replica_groups={{0,1},{2,3},{4,5},{6,7},{8,9},{10,11},{12,13},{14,15},{16,17},{18,19},{..., dimensions={0}, use_global_device_ids=true | all-gather | bytes 786432 | tf_op jit(solution)/shard_map/all_gather | solution.py:221
  18.9 0.0 copy-done.1
  18.9 0.0 copy-done
  18.9 1.7 %image_spectrum.1 = (bf16[2,512,512]{2,1,0:T(8,128)(2,1)S(1)}, f32[2,512]{1,0:T(2,128)S(1)}) custom-call(bf16[2,256,512]{2,1,0:T(8,128)(2,1)S(1)} %all_gather.8.top_ref, bf16[2,256,512]{2,1,0:T(8,128)(2,1)S(1)} %all_gather.9.low_ref, bf16[2,512,512]{2,1,0:T(8,128)(2,1)S(1)} %copy-done, bf16[2,512,512]{2,1,0:T(8,128)(2,1)S(1)} %copy-done.1), custom_call_target="tpu_custom_call" | custom-call | tf_op jit(solution)/shard_map/image_spectrum/pallas_call | solution.py:169
  20.6 0.0 copy-start.2
  20.6 1.0 %copy-done.2 = bf16[2,512,512]{2,1,0:T(8,128)(2,1)} copy-done((bf16[2,512,512]{2,1,0:T(8,128)(2,1)}, bf16[2,512,512]{2,1,0:T(8,128)(2,1)S(1)}, u32[]{:S(2)}) %copy-start.2) | copy-done | bytes 1048600
  21.6 0.2 all-to-all-done.shares_ref
  21.8 0.0 copy-start.3
  21.8 0.2 pick_place.1
  21.9 12.1 %all_to_all.20.shares_ref = bf16[4,2,24,384]{3,2,1,0:T(8,128)(2,1)S(1)} all-to-all(bf16[4,2,24,384]{3,2,1,0:T(8,128)(2,1)S(1)} %pick_place.1), channel_id=1, replica_groups={{4,0,6,2},{5,1,7,3},{12,8,14,10},{13,9,15,11},{20,16,22,18},{21,17,23,1..., dimensions={0} | all-to-all | bytes 294912 | tf_op jit(solution)/shard_map/all_to_all | solution.py:213
  34.1 0.1 pick_plane.1
  34.2 15.8 %all_to_all.21.shares_ref = bf16[16,24,384]{2,1,0:T(8,128)(2,1)S(1)} all-to-all(bf16[16,24,384]{2,1,0:T(8,128)(2,1)S(1)} %pick_plane.1), channel_id=1, replica_groups={{33,32,57,56,17,16,41,40,1,0,25,24,49,48,9,8},{35,34,59,58,19,18,43,42,..., dimensions={0} | all-to-all | bytes 589824 | tf_op jit(solution)/shard_map/all_to_all | solution.py:216
  50.0 0.0 copy-done.3
  50.0 2.3 %correlate.1 = bf16[16,64,512]{2,1,0:T(8,128)(2,1)S(1)} custom-call(bf16[16,24,384]{2,1,0:T(8,128)(2,1)S(1)} %all_to_all.21.shares_ref, bf16[2,512,512]{2,1,0:T(8,128)(2,1)S(1)} %copy-done.3, bf16[2,512,512]{2,1,0:T(8,128)(2,1)S(1)} %copy-done, bf16[2,512,512]{2,1,0:T(8,128)(2,1)S(1)} %copy-done.1), custom_call_target="tpu_custom_call" | custom-call | tf_op jit(solution)/shard_map/correlate/pallas_call | solution.py:169
  52.4 18.7 %all_to_all.22.values_ref = bf16[16,64,512]{2,1,0:T(8,128)(2,1)S(1)} all-to-all(bf16[16,64,512]{2,1,0:T(8,128)(2,1)S(1)} %correlate.1), channel_id=1, replica_groups={{385,129,384,128,449,193,448,192,257,1,256,0,321,65,320,64},{387,131,38..., dimensions={0} | all-to-all | bytes 2097152 | tf_op jit(solution)/shard_map/all_to_all | solution.py:247
  71.0 1.0 %statistics.1 = (f32[1,64,512]{2,1,0:T(8,128)}, f32[1,64,512]{2,1,0:T(8,128)}, f32[1,64,512]{2,1,0:T(8,128)}) custom-call(bf16[16,64,512]{2,1,0:T(8,128)(2,1)S(1)} %all_to_all.22.values_ref, f32[1,512]{1,0:T(1,128)S(1)} %broadcast_select_fusion.level_ref), custom_call_target="tpu_custom_call" | custom-call | tf_op jit(solution)/shard_map/statistics/pallas_call | solution.py:169
  (3 shorter events, 0.1 us)
Async XLA Ops:
  0.6 13.6 %copy-start.4 = (bf16[1,512,512]{2,1,0:T(8,128)(2,1)S(1)}, bf16[1,512,512]{2,1,0:T(8,128)(2,1)}, u32[]{:S(2)}) copy-start(bf16[1,512,512]{2,1,0:T(8,128)(2,1)} %param.5) | copy-start | bytes 1572868
  0.6 21.1 %all-to-all-start = ((bf16[16,24,384]{2,1,0:T(8,128)(2,1)}), bf16[16,24,384]{2,1,0:T(8,128)(2,1)S(1)}, u32[]{:S(2)}, u32[]{:S(2)}) async-start(bf16[16,24,384]{2,1,0:T(8,128)(2,1)} %bitcast.2), calls=%async_computation | async-start | bytes 589824 | tf_op jit(solution)/shard_map/all_to_all | solution.py:207
  14.2 2.5 %copy-start.5 = (s32[1,2]{1,0:T(1,128)S(1)}, s32[1,2]{1,0:T(1,128)}, u32[]{:S(2)}) copy-start(s32[1,2]{1,0:T(1,128)} %param.7) | copy-start | bytes 28
  14.2 4.7 %copy-start.1 = (bf16[2,512,512]{2,1,0:T(8,128)(2,1)S(1)}, bf16[2,512,512]{2,1,0:T(8,128)(2,1)}, u32[]{:S(2)}) copy-start(bf16[2,512,512]{2,1,0:T(8,128)(2,1)} %constant.88.clone.inv_ref) | copy-start | bytes 3145732
  14.3 4.7 %copy-start = (bf16[2,512,512]{2,1,0:T(8,128)(2,1)S(1)}, bf16[2,512,512]{2,1,0:T(8,128)(2,1)}, u32[]{:S(2)}) copy-start(bf16[2,512,512]{2,1,0:T(8,128)(2,1)} %constant.87.clone.fwd_ref) | copy-start | bytes 3145732
  20.6 1.0 %copy-start.2 = (bf16[2,512,512]{2,1,0:T(8,128)(2,1)}, bf16[2,512,512]{2,1,0:T(8,128)(2,1)S(1)}, u32[]{:S(2)}) copy-start(bf16[2,512,512]{2,1,0:T(8,128)(2,1)S(1)} %get-tuple-element.15.spec_ref) | copy-start | bytes 3145732
  21.8 28.2 %copy-start.3 = (bf16[2,512,512]{2,1,0:T(8,128)(2,1)S(1)}, bf16[2,512,512]{2,1,0:T(8,128)(2,1)}, u32[]{:S(2)}) copy-start(bf16[2,512,512]{2,1,0:T(8,128)(2,1)} %copy-done.2) | copy-start | bytes 3145732

commit v9 on v7

--- a/solution.py
+++ b/solution.py
@@ -55,11 +55,9 @@
     return narrow(total)
 
 
-def pick_place_kernel(shares_ref, place_ref, out_ref):
+def pick_kernel(shares_ref, place_ref, out_ref):
     for step in range(STEPS):
-        share = pick(shares_ref, place_ref, step)
-        for receiver in range(out_ref.shape[0]):
-            out_ref[receiver, step] = share
+        out_ref[step] = pick(shares_ref, place_ref, step)
 
 
 def pick_plane_kernel(shares_ref, place_ref, out_ref):
@@ -182,16 +180,12 @@
     return (3 * y + 4) % Y * CORES + 1 - core
 
 
-def column_place(z):
-    return 2 * (z % 2) + 1 - z // 2
-
-
 def plane_members():
     return sorted(((y, c) for y in range(Y) for c in range(CORES)), key=lambda member: plane_place(*member))
 
 
-def column_members():
-    return sorted(range(Z), key=column_place)
+def z_pairs(pairs):
+    return [[(y * Z + z) * CORES + c for z in pair] for pair in pairs for y in range(Y) for c in range(CORES)]
 
 
 def result_members():
@@ -200,20 +194,23 @@
 
 def receive_template(own_template, owners, spec, own_level):
     planes = [[(y * Z + z) * CORES + c for y, c in plane_members()] for z in range(Z)]
-    columns = [[(y * Z + z) * CORES + c for z in column_members()] for y in range(Y) for c in range(CORES)]
-    owner_z = column_place(owners // CORES % Z)
+    owner_z = owners // CORES % Z
     owner_place = plane_place(owners // (Z * CORES), owners % CORES)
-    owner_z, owner_place = (jnp.broadcast_to(place[:, None], (STEPS, M)) for place in (owner_z, owner_place))
+    owner_place, owner_near, owner_far = (
+        jnp.broadcast_to(place[:, None], (STEPS, M)) for place in (owner_place, owner_z % 2, owner_z // 2)
+    )
     shares = own_template.reshape(PLANE, CHUNK, M)
     shares = lax.all_to_all(shares, "tile", 0, 0, axis_index_groups=planes)
-    shares, spec, own_level, owner_z, owner_place = lax.optimization_barrier(
-        (shares, spec, own_level, owner_z, owner_place)
-    )
-    spread = jax.ShapeDtypeStruct((Z, STEPS, CHUNK, M), jnp.bfloat16)
-    shares = call(pick_place_kernel, "pick_place", spread, [], shares, owner_place)
-    shares = lax.all_to_all(shares, "tile", 0, 0, axis_index_groups=columns)
+    shares, spec, own_level, owner_place, owner_near, owner_far = lax.optimization_barrier(
+        (shares, spec, own_level, owner_place, owner_near, owner_far)
+    )
+    kept = jax.ShapeDtypeStruct((STEPS, CHUNK, M), jnp.bfloat16)
+    shares = call(pick_kernel, "pick_place", kept, [], shares, owner_place)
+    shares = lax.all_gather(shares, "tile", axis_index_groups=z_pairs(((0, 1), (2, 3))))
+    shares = call(pick_kernel, "pick_near", kept, [], shares, owner_near)
+    shares = lax.all_gather(shares, "tile", axis_index_groups=z_pairs(((0, 3), (1, 2))))
     spread = jax.ShapeDtypeStruct((PLANE, CHUNK, M), jnp.bfloat16)
-    shares = call(pick_plane_kernel, "pick_plane", spread, [], shares, owner_z)
+    shares = call(pick_plane_kernel, "pick_far", spread, [], shares, owner_far)
     return lax.all_to_all(shares, "tile", 0, 0, axis_index_groups=planes), spec, own_level
 
 

time: 72.4 us -> 73.5 us (1.015)
  blocking collectives: 51.1 us -> 52.1 us
    all_to_all x1 -> x0, blocking collectives: 12 us -> none  [receive_template(): shares = lax.all_to_all(shares, 'tile', 0, 0, axis_index_groups=columns)]
    all_gather x0 -> x2, blocking collectives: none -> 11.6 us  [the longest x1 6.32 us: receive_template(): lax.all_gather(shares, 'tile', axis_index_groups=z_pairs(((0, 3), (1, 2))))]
    all_to_all x1, blocking collectives: 15.8 us -> 16.7 us  [receive_template(): lax.all_to_all(shares, 'tile', 0, 0, axis_index_groups=planes)]
    pallas_call x5 -> x6, Pallas kernels: 5.22 us -> 5.22 us  [call(): pl.pallas_call(kernel, name=name, out_shape=outs, in_specs=[whole] * len(...]
where the time goes in v9:
time: 73.5 us; the launch traced here: 73.2 us
  blocking collectives  52.1 us (71%)
  starting transfers between devices  13.6 us (19%)
  Pallas kernels  5.22 us (7%)
  waiting for transfers between devices  1.21 us (2%)
    all_to_all x1, blocking collectives, per_device(): lax.all_to_all(values, ('orient', 'tile'), 0, 0, axis_index_groups=across)  19.3 us
    all_to_all x1, blocking collectives, receive_template(): lax.all_to_all(shares, 'tile', 0, 0, axis_index_groups=planes)  16.7 us
    all_to_all x1, starting transfers between devices, receive_template(): shares = lax.all_to_all(shares, 'tile', 0, 0, axis_index_groups=planes)  13.6 us
    all_gather x1, blocking collectives, receive_template(): lax.all_gather(shares, 'tile', axis_index_groups=z_pairs(((0, 3), (1, 2))))  6.32 us
    all_gather x1, blocking collectives, receive_template(): lax.all_gather(shares, 'tile', axis_index_groups=z_pairs(((0, 1), (2, 3))))  5.24 us
    pallas_call x6, Pallas kernels, call(): pl.pallas_call(kernel, name=name, out_shape=outs, in_specs=[whole] * len(...  5.22 us
    all_gather x2, blocking collectives, image_fields(): lax.all_gather(half, 'tile', axis_index_groups=pairs)  4.55 us
  transfers between devices with their start and end apart: 1, of which 1 were waited for; matrix products, arithmetic and copies ran while one was open for 0% of the time, Pallas kernels for 2%

profile of v9, /device:TPU:1, one launch (start us, length us, event | category | flops | bytes accessed | tf_op | source)
XLA Modules:
  0.0 73.2 jit_solution(7481474447264858223)
XLA Ops:
  0.6 0.0 copy-start.2
  0.6 13.6 %all-to-all-start = ((bf16[16,24,384]{2,1,0:T(8,128)(2,1)}), bf16[16,24,384]{2,1,0:T(8,128)(2,1)S(1)}, u32[]{:S(2)}, u32[]{:S(2)}) async-start(bf16[16,24,384]{2,1,0:T(8,128)(2,1)} %bitcast.30), calls=%async_computation | async-start | bytes 589824 | tf_op jit(solution)/shard_map/all_to_all | solution.py:203
  14.2 0.0 copy-done.2
  14.2 0.0 copy-start.3
  14.2 0.0 copy-start.1
  14.3 0.0 copy-start
  14.3 2.4 %all_gather.20.top_ref = bf16[2,256,512]{2,1,0:T(8,128)(2,1)S(1)} all-gather(bf16[1,256,512]{2,1,0:T(8,128)(2,1)S(1)} %get-tuple-element.22), channel_id=1, replica_groups={{0,1},{2,3},{4,5},{6,7},{8,9},{10,11},{12,13},{14,15},{16,17},{18,19},{..., dimensions={0}, use_global_device_ids=true | all-gather | bytes 786432 | tf_op jit(solution)/shard_map/all_gather | solution.py:219
  16.7 0.0 copy-done.3
  16.7 2.2 %all_gather.21.low_ref = bf16[2,256,512]{2,1,0:T(8,128)(2,1)S(1)} all-gather(bf16[1,256,512]{2,1,0:T(8,128)(2,1)S(1)} %get-tuple-element.21), channel_id=1, replica_groups={{0,1},{2,3},{4,5},{6,7},{8,9},{10,11},{12,13},{14,15},{16,17},{18,19},{..., dimensions={0}, use_global_device_ids=true | all-gather | bytes 786432 | tf_op jit(solution)/shard_map/all_gather | solution.py:219
  18.9 0.0 copy-done.1
  18.9 0.0 copy-done
  18.9 1.7 %image_spectrum.1 = (bf16[2,512,512]{2,1,0:T(8,128)(2,1)S(1)}, f32[2,512]{1,0:T(2,128)S(1)}) custom-call(bf16[2,256,512]{2,1,0:T(8,128)(2,1)S(1)} %all_gather.20.top_ref, bf16[2,256,512]{2,1,0:T(8,128)(2,1)S(1)} %all_gather.21.low_ref, bf16[2,512,512]{2,1,0:T(8,128)(2,1)S(1)} %copy-done, bf16[2,512,512]{2,1,0:T(8,128)(2,1)S(1)} %copy-done.1), custom_call_target="tpu_custom_call" | custom-call | tf_op jit(solution)/shard_map/image_spectrum/pallas_call | solution.py:168
  20.6 1.2 %all-to-all-done.shares_ref = bf16[16,24,384]{2,1,0:T(8,128)(2,1)S(1)} async-done(((bf16[16,24,384]{2,1,0:T(8,128)(2,1)}), bf16[16,24,384]{2,1,0:T(8,128)(2,1)S(1)}, u32[]{:S(2)}, u32[]{:S(2)}) %all-to-all-start) | async-done | bytes 294944 | tf_op jit(solution)/shard_map/all_to_all | solution.py:203
  21.8 0.1 broadcast_in_dim.7.place_ref
  21.9 0.1 broadcast_in_dim.6.place_ref
  21.9 0.1 broadcast_in_dim.8.place_ref
  22.0 0.1 pick_place.1
  22.1 5.2 %all-gather = bf16[4,24,384]{2,1,0:T(8,128)(2,1)S(1)} all-gather(bf16[2,24,384]{2,1,0:T(8,128)(2,1)S(1)} %pick_place.1), channel_id=2, replica_groups={{0,2},{1,3},{8,10},{9,11},{16,18},{17,19},{24,26},{25,27},{32,34},{33,3..., dimensions={0}, use_global_device_ids=true | all-gather | bytes 110592 | tf_op jit(solution)/shard_map/all_gather | solution.py:209
  27.4 6.3 %all-gather.1 = bf16[4,24,384]{2,1,0:T(8,128)(2,1)S(1)} all-gather(bf16[2,24,384]{2,1,0:T(8,128)(2,1)S(1)} %pick_near.1), channel_id=3, replica_groups={{0,6},{1,7},{8,14},{9,15},{16,22},{17,23},{24,30},{25,31},{32,38},{33,3..., dimensions={0}, use_global_device_ids=true | all-gather | bytes 110592 | tf_op jit(solution)/shard_map/all_gather | solution.py:211
  33.8 16.7 %all_to_all.15.shares_ref = bf16[16,24,384]{2,1,0:T(8,128)(2,1)S(1)} all-to-all(bf16[16,24,384]{2,1,0:T(8,128)(2,1)S(1)} %pick_far.1), channel_id=1, replica_groups={{33,32,57,56,17,16,41,40,1,0,25,24,49,48,9,8},{35,34,59,58,19,18,43,42,..., dimensions={0} | all-to-all | bytes 589824 | tf_op jit(solution)/shard_map/all_to_all | solution.py:214
  50.5 2.3 %correlate.1 = bf16[16,64,512]{2,1,0:T(8,128)(2,1)S(1)} custom-call(bf16[16,24,384]{2,1,0:T(8,128)(2,1)S(1)} %all_to_all.15.shares_ref, bf16[2,512,512]{2,1,0:T(8,128)(2,1)S(1)} %get-tuple-element.17.spec_ref, bf16[2,512,512]{2,1,0:T(8,128)(2,1)S(1)} %copy-done, bf16[2,512,512]{2,1,0:T(8,128)(2,1)S(1)} %copy-done.1), custom_call_target="tpu_custom_call" | custom-call | tf_op jit(solution)/shard_map/correlate/pallas_call | solution.py:168
  52.8 19.3 %all_to_all.16.values_ref = bf16[16,64,512]{2,1,0:T(8,128)(2,1)S(1)} all-to-all(bf16[16,64,512]{2,1,0:T(8,128)(2,1)S(1)} %correlate.1), channel_id=1, replica_groups={{385,129,384,128,449,193,448,192,257,1,256,0,321,65,320,64},{387,131,38..., dimensions={0} | all-to-all | bytes 2097152 | tf_op jit(solution)/shard_map/all_to_all | solution.py:245
  72.1 1.0 %statistics.1 = (f32[1,64,512]{2,1,0:T(8,128)}, f32[1,64,512]{2,1,0:T(8,128)}, f32[1,64,512]{2,1,0:T(8,128)}) custom-call(bf16[16,64,512]{2,1,0:T(8,128)(2,1)S(1)} %all_to_all.16.values_ref, f32[1,512]{1,0:T(1,128)S(1)} %broadcast_select_fusion.level_ref), custom_call_target="tpu_custom_call" | custom-call | tf_op jit(solution)/shard_map/statistics/pallas_call | solution.py:168
  (6 shorter events, 0.1 us)
Async XLA Ops:
  0.6 13.6 %copy-start.2 = (bf16[1,512,512]{2,1,0:T(8,128)(2,1)S(1)}, bf16[1,512,512]{2,1,0:T(8,128)(2,1)}, u32[]{:S(2)}) copy-start(bf16[1,512,512]{2,1,0:T(8,128)(2,1)} %param.5) | copy-start | bytes 1572868
  0.6 21.1 %all-to-all-start = ((bf16[16,24,384]{2,1,0:T(8,128)(2,1)}), bf16[16,24,384]{2,1,0:T(8,128)(2,1)S(1)}, u32[]{:S(2)}, u32[]{:S(2)}) async-start(bf16[16,24,384]{2,1,0:T(8,128)(2,1)} %bitcast.30), calls=%async_computation | async-start | bytes 589824 | tf_op jit(solution)/shard_map/all_to_all | solution.py:203
  14.2 2.5 %copy-start.3 = (s32[1,2]{1,0:T(1,128)S(1)}, s32[1,2]{1,0:T(1,128)}, u32[]{:S(2)}) copy-start(s32[1,2]{1,0:T(1,128)} %param.7) | copy-start | bytes 28
  14.2 4.7 %copy-start.1 = (bf16[2,512,512]{2,1,0:T(8,128)(2,1)S(1)}, bf16[2,512,512]{2,1,0:T(8,128)(2,1)}, u32[]{:S(2)}) copy-start(bf16[2,512,512]{2,1,0:T(8,128)(2,1)} %constant.88.clone.inv_ref) | copy-start | bytes 3145732
  14.3 4.6 %copy-start = (bf16[2,512,512]{2,1,0:T(8,128)(2,1)S(1)}, bf16[2,512,512]{2,1,0:T(8,128)(2,1)}, u32[]{:S(2)}) copy-start(bf16[2,512,512]{2,1,0:T(8,128)(2,1)} %constant.87.clone.fwd_ref) | copy-start | bytes 3145732

commit v10 on v7

--- a/solution.py
+++ b/solution.py
@@ -179,7 +179,7 @@
 
 
 def plane_place(y, core):
-    return (3 * y + 4) % Y * CORES + 1 - core
+    return (5 * y + 4) % Y * CORES + 1 - core
 
 
 def column_place(z):

time: 72.4 us -> 72.5 us (level)
  no operation moved by 1% of the time
where the time goes in v10:
time: 72.5 us; the launch traced here: 72.2 us
  blocking collectives  51.3 us (71%)
  starting transfers between devices  13.6 us (19%)
  Pallas kernels  5.22 us (7%)
  waiting for transfers between devices  1.14 us (2%)
    all_to_all x1, blocking collectives, per_device(): lax.all_to_all(values, ('orient', 'tile'), 0, 0, axis_index_groups=across)  18.7 us
    all_to_all x1, blocking collectives, receive_template(): lax.all_to_all(shares, 'tile', 0, 0, axis_index_groups=planes)  16.1 us
    all_to_all x1, starting transfers between devices, receive_template(): shares = lax.all_to_all(shares, 'tile', 0, 0, axis_index_groups=planes)  13.6 us
    all_to_all x1, blocking collectives, receive_template(): shares = lax.all_to_all(shares, 'tile', 0, 0, axis_index_groups=columns)  12 us
    pallas_call x5, Pallas kernels, call(): pl.pallas_call(kernel, name=name, out_shape=outs, in_specs=[whole] * len(...  5.22 us
    all_gather x2, blocking collectives, image_fields(): lax.all_gather(half, 'tile', axis_index_groups=pairs)  4.54 us
  transfers between devices with their start and end apart: 1, of which 1 were waited for; matrix products, arithmetic and copies ran while one was open for 0% of the time, Pallas kernels for 2%

profile of v10, /device:TPU:1, one launch (start us, length us, event | category | flops | bytes accessed | tf_op | source)
XLA Modules:
  0.0 72.2 jit_solution(10347417502319408914)
XLA Ops:
  0.6 0.0 copy-start.2
  0.6 13.6 %all-to-all-start = ((bf16[16,24,384]{2,1,0:T(8,128)(2,1)}), bf16[16,24,384]{2,1,0:T(8,128)(2,1)S(1)}, u32[]{:S(2)}, u32[]{:S(2)}) async-start(bf16[16,24,384]{2,1,0:T(8,128)(2,1)} %bitcast.25), calls=%async_computation | async-start | bytes 589824 | tf_op jit(solution)/shard_map/all_to_all | solution.py:208
  14.2 0.0 copy-done.2
  14.2 0.0 copy-start.1
  14.3 0.0 copy-start
  14.3 2.4 %all_gather.8.top_ref = bf16[2,256,512]{2,1,0:T(8,128)(2,1)S(1)} all-gather(bf16[1,256,512]{2,1,0:T(8,128)(2,1)S(1)} %get-tuple-element.18), channel_id=1, replica_groups={{0,1},{2,3},{4,5},{6,7},{8,9},{10,11},{12,13},{14,15},{16,17},{18,19},{..., dimensions={0}, use_global_device_ids=true | all-gather | bytes 786432 | tf_op jit(solution)/shard_map/all_gather | solution.py:222
  16.7 2.2 %all_gather.9.low_ref = bf16[2,256,512]{2,1,0:T(8,128)(2,1)S(1)} all-gather(bf16[1,256,512]{2,1,0:T(8,128)(2,1)S(1)} %get-tuple-element.17), channel_id=1, replica_groups={{0,1},{2,3},{4,5},{6,7},{8,9},{10,11},{12,13},{14,15},{16,17},{18,19},{..., dimensions={0}, use_global_device_ids=true | all-gather | bytes 786432 | tf_op jit(solution)/shard_map/all_gather | solution.py:222
  18.8 0.0 copy-done.1
  18.8 0.0 copy-done
  18.8 0.0 copy-start.3
  18.8 1.7 %image_spectrum.1 = (bf16[2,512,512]{2,1,0:T(8,128)(2,1)S(1)}, f32[2,512]{1,0:T(2,128)S(1)}) custom-call(bf16[2,256,512]{2,1,0:T(8,128)(2,1)S(1)} %all_gather.8.top_ref, bf16[2,256,512]{2,1,0:T(8,128)(2,1)S(1)} %all_gather.9.low_ref, bf16[2,512,512]{2,1,0:T(8,128)(2,1)S(1)} %copy-done, bf16[2,512,512]{2,1,0:T(8,128)(2,1)S(1)} %copy-done.1), custom_call_target="tpu_custom_call" | custom-call | tf_op jit(solution)/shard_map/image_spectrum/pallas_call | solution.py:170
  20.5 0.0 copy-done.3
  20.6 1.1 %all-to-all-done.shares_ref = bf16[16,24,384]{2,1,0:T(8,128)(2,1)S(1)} async-done(((bf16[16,24,384]{2,1,0:T(8,128)(2,1)}), bf16[16,24,384]{2,1,0:T(8,128)(2,1)S(1)}, u32[]{:S(2)}, u32[]{:S(2)}) %all-to-all-start) | async-done | bytes 294944 | tf_op jit(solution)/shard_map/all_to_all | solution.py:208
  21.7 0.1 broadcast_in_dim.4.place_ref
  21.8 0.1 broadcast_in_dim.5.place_ref
  21.8 0.1 pick_place.1
  22.0 12.0 %all_to_all.20.shares_ref = bf16[4,2,24,384]{3,2,1,0:T(8,128)(2,1)S(1)} all-to-all(bf16[4,2,24,384]{3,2,1,0:T(8,128)(2,1)S(1)} %pick_place.1), channel_id=1, replica_groups={{4,0,6,2},{5,1,7,3},{12,8,14,10},{13,9,15,11},{20,16,22,18},{21,17,23,1..., dimensions={0} | all-to-all | bytes 294912 | tf_op jit(solution)/shard_map/all_to_all | solution.py:214
  34.0 16.1 %all_to_all.21.shares_ref = bf16[16,24,384]{2,1,0:T(8,128)(2,1)S(1)} all-to-all(bf16[16,24,384]{2,1,0:T(8,128)(2,1)S(1)} %pick_plane.1), channel_id=1, replica_groups={{33,32,9,8,49,48,25,24,1,0,41,40,17,16,57,56},{35,34,11,10,51,50,27,26,..., dimensions={0} | all-to-all | bytes 589824 | tf_op jit(solution)/shard_map/all_to_all | solution.py:217
  50.1 2.3 %correlate.1 = bf16[16,64,512]{2,1,0:T(8,128)(2,1)S(1)} custom-call(bf16[16,24,384]{2,1,0:T(8,128)(2,1)S(1)} %all_to_all.21.shares_ref, bf16[2,512,512]{2,1,0:T(8,128)(2,1)S(1)} %get-tuple-element.15.spec_ref, bf16[2,512,512]{2,1,0:T(8,128)(2,1)S(1)} %copy-done, bf16[2,512,512]{2,1,0:T(8,128)(2,1)S(1)} %copy-done.1), custom_call_target="tpu_custom_call" | custom-call | tf_op jit(solution)/shard_map/correlate/pallas_call | solution.py:170
  52.5 18.7 %all_to_all.22.values_ref = bf16[16,64,512]{2,1,0:T(8,128)(2,1)S(1)} all-to-all(bf16[16,64,512]{2,1,0:T(8,128)(2,1)S(1)} %correlate.1), channel_id=1, replica_groups={{385,129,384,128,449,193,448,192,257,1,256,0,321,65,320,64},{387,131,38..., dimensions={0} | all-to-all | bytes 2097152 | tf_op jit(solution)/shard_map/all_to_all | solution.py:248
  71.1 1.0 %statistics.1 = (f32[1,64,512]{2,1,0:T(8,128)}, f32[1,64,512]{2,1,0:T(8,128)}, f32[1,64,512]{2,1,0:T(8,128)}) custom-call(bf16[16,64,512]{2,1,0:T(8,128)(2,1)S(1)} %all_to_all.22.values_ref, f32[1,512]{1,0:T(1,128)S(1)} %broadcast_select_fusion.level_ref), custom_call_target="tpu_custom_call" | custom-call | tf_op jit(solution)/shard_map/statistics/pallas_call | solution.py:170
  (4 shorter events, 0.1 us)
Async XLA Ops:
  0.6 13.6 %copy-start.2 = (bf16[1,512,512]{2,1,0:T(8,128)(2,1)S(1)}, bf16[1,512,512]{2,1,0:T(8,128)(2,1)}, u32[]{:S(2)}) copy-start(bf16[1,512,512]{2,1,0:T(8,128)(2,1)} %param.5) | copy-start | bytes 1572868
  0.6 21.0 %all-to-all-start = ((bf16[16,24,384]{2,1,0:T(8,128)(2,1)}), bf16[16,24,384]{2,1,0:T(8,128)(2,1)S(1)}, u32[]{:S(2)}, u32[]{:S(2)}) async-start(bf16[16,24,384]{2,1,0:T(8,128)(2,1)} %bitcast.25), calls=%async_computation | async-start | bytes 589824 | tf_op jit(solution)/shard_map/all_to_all | solution.py:208
  14.2 4.6 %copy-start.1 = (bf16[2,512,512]{2,1,0:T(8,128)(2,1)S(1)}, bf16[2,512,512]{2,1,0:T(8,128)(2,1)}, u32[]{:S(2)}) copy-start(bf16[2,512,512]{2,1,0:T(8,128)(2,1)} %constant.89.clone.inv_ref) | copy-start | bytes 3145732
  14.3 4.6 %copy-start = (bf16[2,512,512]{2,1,0:T(8,128)(2,1)S(1)}, bf16[2,512,512]{2,1,0:T(8,128)(2,1)}, u32[]{:S(2)}) copy-start(bf16[2,512,512]{2,1,0:T(8,128)(2,1)} %constant.88.clone.fwd_ref) | copy-start | bytes 3145732
  18.8 1.7 %copy-start.3 = (s32[1,2]{1,0:T(1,128)S(1)}, s32[1,2]{1,0:T(1,128)}, u32[]{:S(2)}) copy-start(s32[1,2]{1,0:T(1,128)} %param.7) | copy-start | bytes 28
